TPU v7x, 32 devices: a whole 2x2x4 slice. The times are simulated.
32 devices in a mesh: rep: 4 (over z), fsdp: 8 (over y, x, core).
Axes of the slice: x: 2, y: 2, z: 4, core: 2. Of those that a mesh axis runs over, the one named last changes fastest.
Arguments:
- tokens: bfloat16 [40960, 1024], P(('rep', 'fsdp')), may hold values from -6 to 6
- item_lengths: int32 [32, 3], P(('rep', 'fsdp')), may hold values from 1 to 1024, 1280 in all within a row
- attn_gain: bfloat16 [1024], P('fsdp'), may hold values from 0.25 to 1.75
- attn_shift: bfloat16 [1024], P('fsdp'), may hold values from -4 to 4
- w_qkv: bfloat16 [1024, 3072], P('fsdp'), may hold values from -0.1875 to 0.1875
- rel_table: bfloat16 [32, 16], P('fsdp'), may hold values from -4 to 4
- w_out: bfloat16 [1024, 1024], P('fsdp'), may hold values from -0.5 to 0.5
- ffn_gain: bfloat16 [1024], P('fsdp'), may hold values from 0.25 to 1.75
- ffn_shift: bfloat16 [1024], P('fsdp'), may hold values from -4 to 4
- w_up: bfloat16 [1024, 4096], P('fsdp'), may hold values from -0.1875 to 0.1875
- up_bias: bfloat16 [4096], P('fsdp'), may hold values from -6 to 6
- w_down: bfloat16 [4096, 1024], P('fsdp'), may hold values from -0.09375 to 0.09375
- down_bias: bfloat16 [1024], P('fsdp'), may hold values from -6 to 6
- cotangent: bfloat16 [40960, 1024], P(('rep', 'fsdp')), may hold values from -6 to 6
Outputs:
- output: bfloat16 [40960, 1024], P(('rep', 'fsdp'))
- grad_tokens: bfloat16 [40960, 1024], P(('rep', 'fsdp'))
- grad_attn_gain: float32 [1024], P('fsdp')
- grad_attn_shift: float32 [1024], P('fsdp')
- grad_w_qkv: float32 [1024, 3072], P('fsdp')
- grad_rel_table: float32 [32, 16], P('fsdp')
- grad_w_out: float32 [1024, 1024], P('fsdp')
- grad_ffn_gain: float32 [1024], P('fsdp')
- grad_ffn_shift: float32 [1024], P('fsdp')
- grad_w_up: float32 [1024, 4096], P('fsdp')
- grad_up_bias: float32 [4096], P('fsdp')
- grad_w_down: float32 [4096, 1024], P('fsdp')
- grad_down_bias: float32 [1024], P('fsdp')
Inputs may be any that keep to these rules, and one draw needn't show every extreme that they name: `item_lengths`: each device's row lists the lengths of its 3 items in order; they sum to 1280 and the longest is exactly 1024.
All inputs are finite; a program needn't handle non-finite values.
Results may differ from a plain program's by a relative error of at most 0.019.
Values may be sent and summed in bfloat16 or wider, within the bound.
No kernel may reach another device: no remote copies, remote signals or barrier semaphores. Data moves between devices by JAX's collectives and lax.ppermute only.
A program may use at most 320 MiB of HBM per device.

v0:
```python
import jax
import jax.numpy as jnp
import numpy as np
from jax import lax
from jax.sharding import PartitionSpec as P

D = 1024
H = 16
HD = 64
NBUCKET = 32
MAXDIST = 128


def layer_norm(values, gain, shift):
    center = values - jnp.mean(values, axis=-1, keepdims=True)
    spread = jnp.mean(center * center, axis=-1, keepdims=True)
    return center * lax.rsqrt(spread + 1e-05) * gain + shift


def gelu_tanh(values):
    return jax.nn.gelu(values, approximate=True)


def bucket_edges(bucket_count, reach_max):
    exact_count = bucket_count // 2
    edge_list = list(range(1, exact_count + 1))
    distance = np.arange(exact_count, 64 * reach_max)
    level_of = exact_count + np.floor(
        np.log(distance / exact_count)
        / np.log(reach_max / exact_count)
        * (bucket_count - exact_count)
    ).astype(np.int64)
    for bucket_id in range(exact_count + 1, bucket_count):
        edge_list.append(int(distance[np.argmax(level_of >= bucket_id)]))
    return edge_list


def bucket_of(distance):
    bucket = jnp.zeros(distance.shape, jnp.int32)
    for edge_value in bucket_edges(NBUCKET, MAXDIST):
        bucket = bucket + (distance >= edge_value).astype(jnp.int32)
    return bucket


def block_masks(positions, seg_ids, row_start, row_stop):
    distance = positions[row_start:row_stop, None] - positions[None, :row_stop]
    allowed = (seg_ids[row_start:row_stop, None] == seg_ids[None, :row_stop]) & (distance >= 0)
    return (bucket_of(distance), allowed)


def block_scores(query_rows, key_rows, table_cols, bucket, allowed):
    scores = (
        jnp.einsum("qhd,khd->hqk", query_rows, key_rows, preferred_element_type=jnp.float32) * 0.125
    )
    for bucket_id in range(NBUCKET):
        scores = scores + jnp.where(
            bucket[None] == bucket_id, table_cols[bucket_id][:, None, None], 0.0
        )
    return jnp.where(allowed[None], scores, -1000000000.0)


def split_heads(columns, head_group):
    row_count = columns.shape[0]
    return jnp.transpose(columns.reshape(row_count, H // head_group, head_group, HD), (1, 0, 2, 3))


def merge_heads(grouped):
    row_count = grouped.shape[1]
    return jnp.transpose(grouped, (1, 0, 2, 3)).reshape(row_count, D)


def local(
    tokens,
    item_lengths,
    attn_gain,
    attn_shift,
    w_qkv,
    rel_table,
    w_out,
    ffn_gain,
    ffn_shift,
    w_up,
    up_bias,
    w_down,
    down_bias,
    cotangent,
):
    gathered = (
        lax.all_gather(attn_gain, "fsdp", axis=0, tiled=True),
        lax.all_gather(attn_shift, "fsdp", axis=0, tiled=True),
        lax.all_gather(w_qkv, "fsdp", axis=0, tiled=True),
        lax.all_gather(rel_table, "fsdp", axis=0, tiled=True),
        lax.all_gather(w_out, "fsdp", axis=0, tiled=True),
        lax.all_gather(ffn_gain, "fsdp", axis=0, tiled=True),
        lax.all_gather(ffn_shift, "fsdp", axis=0, tiled=True),
        lax.all_gather(w_up, "fsdp", axis=0, tiled=True),
        lax.all_gather(up_bias, "fsdp", axis=0, tiled=True),
        lax.all_gather(w_down, "fsdp", axis=0, tiled=True),
        lax.all_gather(down_bias, "fsdp", axis=0, tiled=True),
    )
    (
        gain_one,
        shift_one,
        qkv_full,
        table_full,
        out_full,
        gain_two,
        shift_two,
        up_full,
        up_bias_full,
        down_full,
        down_bias_full,
    ) = gathered
    head_group = 4
    groups = H // head_group
    row_count = tokens.shape[0]
    hidden_in = tokens.astype(jnp.float32)
    item_ends = jnp.cumsum(item_lengths[0])
    positions = jnp.arange(row_count, dtype=jnp.int32)
    seg_ids = jnp.sum((positions[:, None] >= item_ends[None, :]).astype(jnp.int32), axis=1)
    block_rows = row_count // 2
    row_starts = list(range(0, row_count, block_rows))
    normed = layer_norm(
        hidden_in, gain_one.astype(jnp.float32), shift_one.astype(jnp.float32)
    ).astype(jnp.bfloat16)
    packed = jnp.dot(normed, qkv_full, preferred_element_type=jnp.float32).astype(jnp.bfloat16)
    queries = split_heads(packed[:, :D], head_group)
    keys_all = split_heads(packed[:, D : 2 * D], head_group)
    values = split_heads(packed[:, 2 * D :], head_group)
    table_groups = jnp.transpose(
        table_full.astype(jnp.float32).reshape(NBUCKET, groups, head_group), (1, 0, 2)
    )
    mixed_parts = []
    lse_parts = []
    for row_start in row_starts:
        row_stop = row_start + block_rows
        bucket, allowed = block_masks(positions, seg_ids, row_start, row_stop)

        def attend(pieces):
            query_rows, key_rows, value_rows, table_cols = pieces
            scores = block_scores(query_rows, key_rows, table_cols, bucket, allowed)
            row_max = jnp.max(scores, axis=-1, keepdims=True)
            exp_terms = jnp.where(allowed[None], jnp.exp(scores - row_max), 0.0)
            row_total = jnp.sum(exp_terms, axis=-1, keepdims=True)
            probs_low = (exp_terms / row_total).astype(jnp.bfloat16)
            attended_rows = jnp.einsum(
                "hqk,khd->qhd", probs_low, value_rows, preferred_element_type=jnp.float32
            )
            return (attended_rows, (row_max + jnp.log(row_total))[..., 0])

        block_out, block_lse = lax.map(
            attend,
            (
                queries[:, row_start:row_stop],
                keys_all[:, :row_stop],
                values[:, :row_stop],
                table_groups,
            ),
        )
        mixed_parts.append(jnp.transpose(block_out, (1, 0, 2, 3)).reshape(block_rows, D))
        lse_parts.append(block_lse)
    mixed = jnp.concatenate(mixed_parts, axis=0).astype(jnp.bfloat16)
    middle = hidden_in + jnp.dot(mixed, out_full, preferred_element_type=jnp.float32)
    normed_two = layer_norm(
        middle, gain_two.astype(jnp.float32), shift_two.astype(jnp.float32)
    ).astype(jnp.bfloat16)
    pre_act = jnp.dot(
        normed_two, up_full, preferred_element_type=jnp.float32
    ) + up_bias_full.astype(jnp.float32)
    activ = gelu_tanh(pre_act).astype(jnp.bfloat16)
    ffn_out = jnp.dot(activ, down_full, preferred_element_type=jnp.float32) + down_bias_full.astype(
        jnp.float32
    )
    output = (middle + ffn_out).astype(jnp.bfloat16)
    back_weights = (
        lax.all_gather(attn_gain, "fsdp", axis=0, tiled=True),
        lax.all_gather(attn_shift, "fsdp", axis=0, tiled=True),
        lax.all_gather(w_qkv, "fsdp", axis=0, tiled=True),
        lax.all_gather(rel_table, "fsdp", axis=0, tiled=True),
        lax.all_gather(w_out, "fsdp", axis=0, tiled=True),
        lax.all_gather(ffn_gain, "fsdp", axis=0, tiled=True),
        lax.all_gather(ffn_shift, "fsdp", axis=0, tiled=True),
        lax.all_gather(w_up, "fsdp", axis=0, tiled=True),
        lax.all_gather(up_bias, "fsdp", axis=0, tiled=True),
        lax.all_gather(w_down, "fsdp", axis=0, tiled=True),
        lax.all_gather(down_bias, "fsdp", axis=0, tiled=True),
    )
    (
        gain_one_b,
        shift_one_b,
        qkv_back,
        table_back,
        out_back,
        gain_two_b,
        shift_two_b,
        up_back,
        up_bias_back,
        down_back,
        down_bias_back,
    ) = back_weights
    table_back_groups = jnp.transpose(
        table_back.astype(jnp.float32).reshape(NBUCKET, groups, head_group), (1, 0, 2)
    )
    cot_float = cotangent.astype(jnp.float32)
    grad_w_down = jnp.einsum("tf,td->fd", activ, cotangent, preferred_element_type=jnp.float32)
    grad_down_bias = jnp.sum(cot_float, axis=0)
    grad_activ = jnp.einsum("td,fd->tf", cotangent, down_back, preferred_element_type=jnp.float32)
    gelu_value, gelu_back = jax.vjp(gelu_tanh, pre_act)
    grad_pre = gelu_back(grad_activ)[0].astype(jnp.bfloat16)
    grad_w_up = jnp.einsum("td,tf->df", normed_two, grad_pre, preferred_element_type=jnp.float32)
    grad_up_bias = jnp.sum(grad_pre.astype(jnp.float32), axis=0)
    grad_normed_two = jnp.einsum("tf,df->td", grad_pre, up_back, preferred_element_type=jnp.float32)
    norm_value, norm_back = jax.vjp(
        layer_norm, middle, gain_two_b.astype(jnp.float32), shift_two_b.astype(jnp.float32)
    )
    grad_mid_norm, grad_ffn_gain, grad_ffn_shift = norm_back(grad_normed_two)
    grad_middle = cot_float + grad_mid_norm
    grad_attended = grad_middle.astype(jnp.bfloat16)
    grad_w_out = jnp.einsum("td,te->de", mixed, grad_attended, preferred_element_type=jnp.float32)
    grad_mixed = jnp.einsum(
        "te,de->td", grad_attended, out_back, preferred_element_type=jnp.float32
    ).astype(jnp.bfloat16)
    grad_mixed_heads = split_heads(grad_mixed, head_group)
    grad_query_parts = []
    grad_keys_sum = jnp.zeros((groups, row_count, head_group, HD), jnp.float32)
    grad_values_sum = jnp.zeros((groups, row_count, head_group, HD), jnp.float32)
    grad_table_sum = jnp.zeros((groups, NBUCKET, head_group), jnp.float32)
    for block_number, row_start in enumerate(row_starts):
        row_stop = row_start + block_rows
        bucket, allowed = block_masks(positions, seg_ids, row_start, row_stop)

        def attend_back(pieces):
            query_rows, key_rows, value_rows, table_cols, lse_rows, grad_rows = pieces
            scores = block_scores(query_rows, key_rows, table_cols, bucket, allowed)
            probs = jnp.where(allowed[None], jnp.exp(scores - lse_rows[..., None]), 0.0)
            grad_probs = jnp.einsum(
                "qhd,khd->hqk", grad_rows, value_rows, preferred_element_type=jnp.float32
            )
            inner = jnp.sum(probs * grad_probs, axis=-1, keepdims=True)
            grad_scores = (probs * (grad_probs - inner)).astype(jnp.bfloat16)
            grad_value_rows = jnp.einsum(
                "hqk,qhd->khd",
                probs.astype(jnp.bfloat16),
                grad_rows,
                preferred_element_type=jnp.float32,
            )
            grad_query_rows = (
                jnp.einsum(
                    "hqk,khd->qhd", grad_scores, key_rows, preferred_element_type=jnp.float32
                )
                * 0.125
            )
            grad_key_rows = (
                jnp.einsum(
                    "hqk,qhd->khd", grad_scores, query_rows, preferred_element_type=jnp.float32
                )
                * 0.125
            )
            grad_float = grad_scores.astype(jnp.float32)
            table_rows = [
                jnp.sum(jnp.where(bucket[None] == bucket_id, grad_float, 0.0), axis=(1, 2))
                for bucket_id in range(NBUCKET)
            ]
            return (grad_query_rows, grad_key_rows, grad_value_rows, jnp.stack(table_rows, axis=0))

        block_query, block_key, block_value, block_table = lax.map(
            attend_back,
            (
                queries[:, row_start:row_stop],
                keys_all[:, :row_stop],
                values[:, :row_stop],
                table_back_groups,
                lse_parts[block_number],
                grad_mixed_heads[:, row_start:row_stop],
            ),
        )
        grad_query_parts.append(block_query)
        padding = ((0, 0), (0, row_count - row_stop), (0, 0), (0, 0))
        grad_keys_sum = grad_keys_sum + jnp.pad(block_key, padding)
        grad_values_sum = grad_values_sum + jnp.pad(block_value, padding)
        grad_table_sum = grad_table_sum + block_table
    grad_queries = jnp.concatenate(grad_query_parts, axis=1)
    grad_packed = jnp.concatenate(
        [merge_heads(grad_queries), merge_heads(grad_keys_sum), merge_heads(grad_values_sum)],
        axis=1,
    ).astype(jnp.bfloat16)
    grad_rel_table = jnp.transpose(grad_table_sum, (1, 0, 2)).reshape(NBUCKET, H)
    grad_w_qkv = jnp.einsum("td,te->de", normed, grad_packed, preferred_element_type=jnp.float32)
    grad_normed = jnp.einsum("te,de->td", grad_packed, qkv_back, preferred_element_type=jnp.float32)
    first_value, first_back = jax.vjp(
        layer_norm, hidden_in, gain_one_b.astype(jnp.float32), shift_one_b.astype(jnp.float32)
    )
    grad_in_norm, grad_attn_gain, grad_attn_shift = first_back(grad_normed)
    grad_tokens = (grad_middle + grad_in_norm).astype(jnp.bfloat16)
    shares = (
        lax.psum_scatter(
            grad_attn_gain.astype(jnp.bfloat16), "fsdp", scatter_dimension=0, tiled=True
        ).astype(jnp.float32),
        lax.psum_scatter(
            grad_attn_shift.astype(jnp.bfloat16), "fsdp", scatter_dimension=0, tiled=True
        ).astype(jnp.float32),
        lax.psum_scatter(
            grad_w_qkv.astype(jnp.bfloat16), "fsdp", scatter_dimension=0, tiled=True
        ).astype(jnp.float32),
        lax.psum_scatter(
            grad_rel_table.astype(jnp.bfloat16), "fsdp", scatter_dimension=0, tiled=True
        ).astype(jnp.float32),
        lax.psum_scatter(
            grad_w_out.astype(jnp.bfloat16), "fsdp", scatter_dimension=0, tiled=True
        ).astype(jnp.float32),
        lax.psum_scatter(
            grad_ffn_gain.astype(jnp.bfloat16), "fsdp", scatter_dimension=0, tiled=True
        ).astype(jnp.float32),
        lax.psum_scatter(
            grad_ffn_shift.astype(jnp.bfloat16), "fsdp", scatter_dimension=0, tiled=True
        ).astype(jnp.float32),
        lax.psum_scatter(
            grad_w_up.astype(jnp.bfloat16), "fsdp", scatter_dimension=0, tiled=True
        ).astype(jnp.float32),
        lax.psum_scatter(
            grad_up_bias.astype(jnp.bfloat16), "fsdp", scatter_dimension=0, tiled=True
        ).astype(jnp.float32),
        lax.psum_scatter(
            grad_w_down.astype(jnp.bfloat16), "fsdp", scatter_dimension=0, tiled=True
        ).astype(jnp.float32),
        lax.psum_scatter(
            grad_down_bias.astype(jnp.bfloat16), "fsdp", scatter_dimension=0, tiled=True
        ).astype(jnp.float32),
    )
    (
        share_attn_gain,
        share_attn_shift,
        share_qkv,
        share_table,
        share_out,
        share_ffn_gain,
        share_ffn_shift,
        share_up,
        share_up_bias,
        share_down,
        share_down_bias,
    ) = shares
    summed = (
        lax.psum(share_attn_gain.astype(jnp.bfloat16), "rep").astype(jnp.float32),
        lax.psum(share_attn_shift.astype(jnp.bfloat16), "rep").astype(jnp.float32),
        lax.psum(share_qkv.astype(jnp.bfloat16), "rep").astype(jnp.float32),
        lax.psum(share_table.astype(jnp.bfloat16), "rep").astype(jnp.float32),
        lax.psum(share_out.astype(jnp.bfloat16), "rep").astype(jnp.float32),
        lax.psum(share_ffn_gain.astype(jnp.bfloat16), "rep").astype(jnp.float32),
        lax.psum(share_ffn_shift.astype(jnp.bfloat16), "rep").astype(jnp.float32),
        lax.psum(share_up.astype(jnp.bfloat16), "rep").astype(jnp.float32),
        lax.psum(share_up_bias.astype(jnp.bfloat16), "rep").astype(jnp.float32),
        lax.psum(share_down.astype(jnp.bfloat16), "rep").astype(jnp.float32),
        lax.psum(share_down_bias.astype(jnp.bfloat16), "rep").astype(jnp.float32),
    )
    return (output, grad_tokens) + tuple(summed)


def solution(mesh):
    in_specs = (
        P(("rep", "fsdp"), None),
        P(("rep", "fsdp"), None),
        P("fsdp"),
        P("fsdp"),
        P("fsdp", None),
        P("fsdp", None),
        P("fsdp", None),
        P("fsdp"),
        P("fsdp"),
        P("fsdp", None),
        P("fsdp"),
        P("fsdp", None),
        P("fsdp"),
        P(("rep", "fsdp"), None),
    )
    out_specs = (
        P(("rep", "fsdp"), None),
        P(("rep", "fsdp"), None),
        P("fsdp"),
        P("fsdp"),
        P("fsdp", None),
        P("fsdp", None),
        P("fsdp", None),
        P("fsdp"),
        P("fsdp"),
        P("fsdp", None),
        P("fsdp"),
        P("fsdp", None),
        P("fsdp"),
    )
    return jax.shard_map(local, mesh=mesh, in_specs=in_specs, out_specs=out_specs, check_vma=False)
```

profile of v0, /device:TPU:0, one launch (start us, length us, event | category | flops | bytes accessed | tf_op | source)
XLA Modules:
  0.0 2339.4 jit_solution(17940204499433741773)
XLA Ops:
  131.9 373.9 %while.69 = (s32[]{:T(128)}, bf16[4,640,4,64]{1,3,2,0:T(8,128)(2,1)}, f32[4,4,640]{2,1,0:T(4,128)}, bf16[4,1280,4,64]{1,3,2,0:T(8,128)(2,1)}, bf16[4,640,4,64]{1...) while((s32[]{:T(128)}, ...), condition=%wide.region_11.12_spmd.clone.clone.clone, body=%wide.region_8.11_spmd.clone.clone.sunk.clone | while | flops 1110832640 | bytes 137492976 | solution.py:151
  133.2 17.8 broadcast_compare_fusion.137
  151.1 56.9 %fusion.499 = (f32[4,640]{1,0:T(4,128)S(1)}, f32[4,640,1280]{2,1,0:T(8,128)}) fusion(f32[4]{0:T(128)S(1)} %get-tuple-element.3068, pred[640,1280]{1,0:T(8,128)(4,1)S(1)} %get-tuple-element.3069, f32[4]{0:T(128)S(1)} %get-tuple-element.3070, pred[640,1280]{1,0:T(8,128)(4,1)S(1)} %get-tuple-element.3071, f32[4]{0:T(128)S(1)} %get-tuple-element.3072, ...), kind=kOutput, calls=%fused_computation.767.clone.1.clone | convolution fusion | flops 638973440 | bytes 41135616 | tf_op jit(solution)/shard_map/while/body/eval_jaxpr/qhd,khd->hqk/dot_general | solution.py:53
  226.9 17.8 broadcast_compare_fusion.137
  244.8 56.5 %fusion.499 = (f32[4,640]{1,0:T(4,128)S(1)}, f32[4,640,1280]{2,1,0:T(8,128)}) fusion(f32[4]{0:T(128)S(1)} %get-tuple-element.3068, pred[640,1280]{1,0:T(8,128)(4,1)S(1)} %get-tuple-element.3069, f32[4]{0:T(128)S(1)} %get-tuple-element.3070, pred[640,1280]{1,0:T(8,128)(4,1)S(1)} %get-tuple-element.3071, f32[4]{0:T(128)S(1)} %get-tuple-element.3072, ...), kind=kOutput, calls=%fused_computation.767.clone.1.clone | convolution fusion | flops 638973440 | bytes 41135616 | tf_op jit(solution)/shard_map/while/body/eval_jaxpr/qhd,khd->hqk/dot_general | solution.py:53
  320.1 17.8 broadcast_compare_fusion.137
  338.0 56.5 %fusion.499 = (f32[4,640]{1,0:T(4,128)S(1)}, f32[4,640,1280]{2,1,0:T(8,128)}) fusion(f32[4]{0:T(128)S(1)} %get-tuple-element.3068, pred[640,1280]{1,0:T(8,128)(4,1)S(1)} %get-tuple-element.3069, f32[4]{0:T(128)S(1)} %get-tuple-element.3070, pred[640,1280]{1,0:T(8,128)(4,1)S(1)} %get-tuple-element.3071, f32[4]{0:T(128)S(1)} %get-tuple-element.3072, ...), kind=kOutput, calls=%fused_computation.767.clone.1.clone | convolution fusion | flops 638973440 | bytes 41135616 | tf_op jit(solution)/shard_map/while/body/eval_jaxpr/qhd,khd->hqk/dot_general | solution.py:53
  431.3 56.5 %fusion.499 = (f32[4,640]{1,0:T(4,128)S(1)}, f32[4,640,1280]{2,1,0:T(8,128)}) fusion(f32[4]{0:T(128)S(1)} %get-tuple-element.3068, pred[640,1280]{1,0:T(8,128)(4,1)S(1)} %get-tuple-element.3069, f32[4]{0:T(128)S(1)} %get-tuple-element.3070, pred[640,1280]{1,0:T(8,128)(4,1)S(1)} %get-tuple-element.3071, f32[4]{0:T(128)S(1)} %get-tuple-element.3072, ...), kind=kOutput, calls=%fused_computation.767.clone.1.clone | convolution fusion | flops 638973440 | bytes 41135616 | tf_op jit(solution)/shard_map/while/body/eval_jaxpr/qhd,khd->hqk/dot_general | solution.py:53
  507.6 183.0 %while.68 = (s32[]{:T(128)}, bf16[4,640,4,64]{1,3,2,0:T(8,128)(2,1)}, f32[4,4,640]{2,1,0:T(4,128)S(1)}, bf16[4,640,4,64]{1,3,2,0:T(8,128)(2,1)}, bf16[4,640,4,64...) while((s32[]{:T(128)}, ...), condition=%wide.region_7.8_spmd.clone.clone.clone, body=%wide.region_4.7_spmd.clone.clone.sunk.clone | while | flops 555415040 | bytes 61367456 | solution.py:151
  519.2 28.9 %fusion.492 = (f32[4,640]{1,0:T(4,128)S(1)}, f32[4,640,640]{1,2,0:T(8,128)S(1)}) fusion(f32[4]{0:T(128)S(1)} %get-tuple-element.2947, pred[640,640]{0,1:T(8,128)(4,1)S(1)} %get-tuple-element.2948, f32[4]{0:T(128)S(1)} %get-tuple-element.2949, pred[640,640]{0,1:T(8,128)(4,1)S(1)} %get-tuple-element.2950, f32[4]{0:T(128)S(1)} %get-tuple-element.2951, ...), kind=kOutput, calls=%fused_computation.766.clone.1.clone | convolution fusion | flops 319485440 | bytes 20737536 | tf_op jit(solution)/shard_map/while/body/eval_jaxpr/qhd,khd->hqk/dot_general | solution.py:53
  564.9 28.9 %fusion.492 = (f32[4,640]{1,0:T(4,128)S(1)}, f32[4,640,640]{1,2,0:T(8,128)S(1)}) fusion(f32[4]{0:T(128)S(1)} %get-tuple-element.2947, pred[640,640]{0,1:T(8,128)(4,1)S(1)} %get-tuple-element.2948, f32[4]{0:T(128)S(1)} %get-tuple-element.2949, pred[640,640]{0,1:T(8,128)(4,1)S(1)} %get-tuple-element.2950, f32[4]{0:T(128)S(1)} %get-tuple-element.2951, ...), kind=kOutput, calls=%fused_computation.766.clone.1.clone | convolution fusion | flops 319485440 | bytes 20737536 | tf_op jit(solution)/shard_map/while/body/eval_jaxpr/qhd,khd->hqk/dot_general | solution.py:53
  610.6 28.9 %fusion.492 = (f32[4,640]{1,0:T(4,128)S(1)}, f32[4,640,640]{1,2,0:T(8,128)S(1)}) fusion(f32[4]{0:T(128)S(1)} %get-tuple-element.2947, pred[640,640]{0,1:T(8,128)(4,1)S(1)} %get-tuple-element.2948, f32[4]{0:T(128)S(1)} %get-tuple-element.2949, pred[640,640]{0,1:T(8,128)(4,1)S(1)} %get-tuple-element.2950, f32[4]{0:T(128)S(1)} %get-tuple-element.2951, ...), kind=kOutput, calls=%fused_computation.766.clone.1.clone | convolution fusion | flops 319485440 | bytes 20737536 | tf_op jit(solution)/shard_map/while/body/eval_jaxpr/qhd,khd->hqk/dot_general | solution.py:53
  656.3 28.9 %fusion.492 = (f32[4,640]{1,0:T(4,128)S(1)}, f32[4,640,640]{1,2,0:T(8,128)S(1)}) fusion(f32[4]{0:T(128)S(1)} %get-tuple-element.2947, pred[640,640]{0,1:T(8,128)(4,1)S(1)} %get-tuple-element.2948, f32[4]{0:T(128)S(1)} %get-tuple-element.2949, pred[640,640]{0,1:T(8,128)(4,1)S(1)} %get-tuple-element.2950, f32[4]{0:T(128)S(1)} %get-tuple-element.2951, ...), kind=kOutput, calls=%fused_computation.766.clone.1.clone | convolution fusion | flops 319485440 | bytes 20737536 | tf_op jit(solution)/shard_map/while/body/eval_jaxpr/qhd,khd->hqk/dot_general | solution.py:53
  700.3 19.9 fusion.356
  720.2 30.3 %fusion.357 = (bf16[4096]{0:T(1024)(128)(2,1)}, bf16[1280,4096]{1,0:T(8,128)(2,1)}) fusion(f32[1280,4096]{1,0:T(8,128)} %fusion.356, f32[4096]{0:T(1024)S(1)} %bitcast.948, bf16[1280,1024]{1,0:T(8,128)(2,1)S(1)} %copy-done.39, bf16[4096,1024]{1,0:T(8,128)(2,1)} %all-gather.18.cloned.1.call-done), kind=kOutput, calls=%fused_computation.764 | convolution fusion | flops 10852757504 | bytes 42491904 | tf_op jit(solution)/shard_map/td,fd->tf/dot_general | solution.py:207
  794.5 350.5 %while.70 = (s32[]{:T(128)}, bf16[4,640,4,64]{1,3,2,0:T(8,128)(2,1)}, f32[4,640,4,64]{1,3,2,0:T(8,128)}, f32[4,640,4,64]{1,3,2,0:T(8,128)}, f32[4,32,4]{1,2,0:T(...) while((s32[]{:T(128)}, ...), condition=%wide.region_50.51_spmd.clone.clone.clone, body=%wide.region_16.50_spmd.clone.clone.sunk.clone | while | flops 1293022720 | bytes 98538120 | solution.py:266
  808.6 30.7 %multiply_reduce_fusion.9 = (f32[4,640]{1,0:T(4,128)S(1)}, f32[4,640,640]{1,2,0:T(8,128)S(1)}) fusion(f32[4,640,640]{1,2,0:T(8,128)S(1)} %fusion.510, f32[4,640]{1,0:T(4,128)S(1)} %fusion.511, f32[4]{0:T(128)S(1)} %get-tuple-element.3211, pred[640,640]{0,1:T(8,128)(4,1)S(1)} %get-tuple-element.3193, f32[4]{0:T(128)S(1)} %get-tuple-element.3212, ...), kind=kOutput, calls=%fused_computation.299.clone.1.clone | convolution fusion | flops 324400640 | bytes 27301376 | tf_op jit(solution)/shard_map/while/body/eval_jaxpr/qhd,khd->hqk/dot_general | solution.py:53
  839.2 18.3 fusion.515
  896.1 30.7 %multiply_reduce_fusion.9 = (f32[4,640]{1,0:T(4,128)S(1)}, f32[4,640,640]{1,2,0:T(8,128)S(1)}) fusion(f32[4,640,640]{1,2,0:T(8,128)S(1)} %fusion.510, f32[4,640]{1,0:T(4,128)S(1)} %fusion.511, f32[4]{0:T(128)S(1)} %get-tuple-element.3211, pred[640,640]{0,1:T(8,128)(4,1)S(1)} %get-tuple-element.3193, f32[4]{0:T(128)S(1)} %get-tuple-element.3212, ...), kind=kOutput, calls=%fused_computation.299.clone.1.clone | convolution fusion | flops 324400640 | bytes 27301376 | tf_op jit(solution)/shard_map/while/body/eval_jaxpr/qhd,khd->hqk/dot_general | solution.py:53
  926.8 18.3 fusion.515
  983.6 30.7 %multiply_reduce_fusion.9 = (f32[4,640]{1,0:T(4,128)S(1)}, f32[4,640,640]{1,2,0:T(8,128)S(1)}) fusion(f32[4,640,640]{1,2,0:T(8,128)S(1)} %fusion.510, f32[4,640]{1,0:T(4,128)S(1)} %fusion.511, f32[4]{0:T(128)S(1)} %get-tuple-element.3211, pred[640,640]{0,1:T(8,128)(4,1)S(1)} %get-tuple-element.3193, f32[4]{0:T(128)S(1)} %get-tuple-element.3212, ...), kind=kOutput, calls=%fused_computation.299.clone.1.clone | convolution fusion | flops 324400640 | bytes 27301376 | tf_op jit(solution)/shard_map/while/body/eval_jaxpr/qhd,khd->hqk/dot_general | solution.py:53
  1014.3 18.3 fusion.515
  1071.2 30.7 %multiply_reduce_fusion.9 = (f32[4,640]{1,0:T(4,128)S(1)}, f32[4,640,640]{1,2,0:T(8,128)S(1)}) fusion(f32[4,640,640]{1,2,0:T(8,128)S(1)} %fusion.510, f32[4,640]{1,0:T(4,128)S(1)} %fusion.511, f32[4]{0:T(128)S(1)} %get-tuple-element.3211, pred[640,640]{0,1:T(8,128)(4,1)S(1)} %get-tuple-element.3193, f32[4]{0:T(128)S(1)} %get-tuple-element.3212, ...), kind=kOutput, calls=%fused_computation.299.clone.1.clone | convolution fusion | flops 324400640 | bytes 27301376 | tf_op jit(solution)/shard_map/while/body/eval_jaxpr/qhd,khd->hqk/dot_general | solution.py:53
  1101.9 18.3 fusion.515
  1145.6 796.4 %while.71 = (s32[]{:T(128)}, bf16[4,640,4,64]{1,3,2,0:T(8,128)(2,1)}, f32[4,1280,4,64]{1,3,2,0:T(8,128)}, f32[4,1280,4,64]{1,3,2,0:T(8,128)}, f32[4,32,4]{1,2,0:...) while((s32[]{:T(128)}, ...), condition=%wide.region_85.86_spmd.clone.clone.clone, body=%wide.region_51.85_spmd.clone.clone.sunk.clone | while | flops 2585884160 | bytes 343230208 | solution.py:266
  1175.0 18.6 broadcast_compare_fusion.139
  1193.7 64.7 %multiply_reduce_fusion.10 = (f32[4,640]{1,0:T(4,128)S(1)}, f32[4,640,1280]{2,1,0:T(8,128)}) fusion(f32[4,640,1280]{2,1,0:T(8,128)} %fusion.528, f32[4,640]{1,0:T(4,128)} %fusion.529, f32[4]{0:T(128)} %get-tuple-element.3373, pred[640,1280]{1,0:T(8,128)(4,1)S(1)} %get-tuple-element.3355, f32[4]{0:T(128)} %get-tuple-element.3374, ...), kind=kOutput, calls=%fused_computation.497.clone.3.clone | convolution fusion | flops 648803840 | bytes 54268432 | tf_op jit(solution)/shard_map/while/body/eval_jaxpr/qhd,khd->hqk/dot_general | solution.py:53
  1258.5 48.4 %fusion.533 = (f32[4]{0:T(128)S(1)}, f32[4]{0:T(128)}, f32[4]{0:T(128)}, f32[4]{0:T(128)}, f32[4]{0:T(128)}, /*index=5*/f32[4]{0:T(128)}, f32[4]{0:T(128)}, f32[...) fusion(pred[640,1280]{1,0:T(8,128)(4,1)S(1)} %get-tuple-element, ...), kind=kLoop, calls=%fused_computation.495.clone.1.clone | loop fusion | flops 131071968 | bytes 47524128 | tf_op jit(solution)/shard_map/while/body/eval_jaxpr/reduce_sum | solution.py:261
  1317.9 26.4 %fusion.537 = (f32[4]{0:T(128)S(1)}, f32[4]{0:T(128)S(1)}, f32[4]{0:T(128)S(1)}, f32[4]{0:T(128)S(1)}, f32[4]{0:T(128)S(1)}, /*index=5*/f32[4]{0:T(128)S(1)}, f3...) fusion(bf16[4,640,1280]{2,1,0:T(8,128)(2,1)S(1)} %get-tuple-ele, ...), kind=kLoop, calls=%fused_computation.494.clone.1.clone | loop fusion | flops 95027152 | bytes 18022624 | tf_op jit(solution)/shard_map/while/body/eval_jaxpr/reduce_sum | solution.py:261
  1369.7 18.6 broadcast_compare_fusion.139
  1388.4 64.7 %multiply_reduce_fusion.10 = (f32[4,640]{1,0:T(4,128)S(1)}, f32[4,640,1280]{2,1,0:T(8,128)}) fusion(f32[4,640,1280]{2,1,0:T(8,128)} %fusion.528, f32[4,640]{1,0:T(4,128)} %fusion.529, f32[4]{0:T(128)} %get-tuple-element.3373, pred[640,1280]{1,0:T(8,128)(4,1)S(1)} %get-tuple-element.3355, f32[4]{0:T(128)} %get-tuple-element.3374, ...), kind=kOutput, calls=%fused_computation.497.clone.3.clone | convolution fusion | flops 648803840 | bytes 54268432 | tf_op jit(solution)/shard_map/while/body/eval_jaxpr/qhd,khd->hqk/dot_general | solution.py:53
  1453.2 48.4 %fusion.533 = (f32[4]{0:T(128)S(1)}, f32[4]{0:T(128)}, f32[4]{0:T(128)}, f32[4]{0:T(128)}, f32[4]{0:T(128)}, /*index=5*/f32[4]{0:T(128)}, f32[4]{0:T(128)}, f32[...) fusion(pred[640,1280]{1,0:T(8,128)(4,1)S(1)} %get-tuple-element, ...), kind=kLoop, calls=%fused_computation.495.clone.1.clone | loop fusion | flops 131071968 | bytes 47524128 | tf_op jit(solution)/shard_map/while/body/eval_jaxpr/reduce_sum | solution.py:261
  1512.7 26.4 %fusion.537 = (f32[4]{0:T(128)S(1)}, f32[4]{0:T(128)S(1)}, f32[4]{0:T(128)S(1)}, f32[4]{0:T(128)S(1)}, f32[4]{0:T(128)S(1)}, /*index=5*/f32[4]{0:T(128)S(1)}, f3...) fusion(bf16[4,640,1280]{2,1,0:T(8,128)(2,1)S(1)} %get-tuple-ele, ...), kind=kLoop, calls=%fused_computation.494.clone.1.clone | loop fusion | flops 95027152 | bytes 18022624 | tf_op jit(solution)/shard_map/while/body/eval_jaxpr/reduce_sum | solution.py:261
  1564.5 18.6 broadcast_compare_fusion.139
  1583.2 64.7 %multiply_reduce_fusion.10 = (f32[4,640]{1,0:T(4,128)S(1)}, f32[4,640,1280]{2,1,0:T(8,128)}) fusion(f32[4,640,1280]{2,1,0:T(8,128)} %fusion.528, f32[4,640]{1,0:T(4,128)} %fusion.529, f32[4]{0:T(128)} %get-tuple-element.3373, pred[640,1280]{1,0:T(8,128)(4,1)S(1)} %get-tuple-element.3355, f32[4]{0:T(128)} %get-tuple-element.3374, ...), kind=kOutput, calls=%fused_computation.497.clone.3.clone | convolution fusion | flops 648803840 | bytes 54268432 | tf_op jit(solution)/shard_map/while/body/eval_jaxpr/qhd,khd->hqk/dot_general | solution.py:53
  1648.0 48.4 %fusion.533 = (f32[4]{0:T(128)S(1)}, f32[4]{0:T(128)}, f32[4]{0:T(128)}, f32[4]{0:T(128)}, f32[4]{0:T(128)}, /*index=5*/f32[4]{0:T(128)}, f32[4]{0:T(128)}, f32[...) fusion(pred[640,1280]{1,0:T(8,128)(4,1)S(1)} %get-tuple-element, ...), kind=kLoop, calls=%fused_computation.495.clone.1.clone | loop fusion | flops 131071968 | bytes 47524128 | tf_op jit(solution)/shard_map/while/body/eval_jaxpr/reduce_sum | solution.py:261
  1707.4 26.4 %fusion.537 = (f32[4]{0:T(128)S(1)}, f32[4]{0:T(128)S(1)}, f32[4]{0:T(128)S(1)}, f32[4]{0:T(128)S(1)}, f32[4]{0:T(128)S(1)}, /*index=5*/f32[4]{0:T(128)S(1)}, f3...) fusion(bf16[4,640,1280]{2,1,0:T(8,128)(2,1)S(1)} %get-tuple-ele, ...), kind=kLoop, calls=%fused_computation.494.clone.1.clone | loop fusion | flops 95027152 | bytes 18022624 | tf_op jit(solution)/shard_map/while/body/eval_jaxpr/reduce_sum | solution.py:261
  1759.2 18.6 broadcast_compare_fusion.139
  1777.9 64.7 %multiply_reduce_fusion.10 = (f32[4,640]{1,0:T(4,128)S(1)}, f32[4,640,1280]{2,1,0:T(8,128)}) fusion(f32[4,640,1280]{2,1,0:T(8,128)} %fusion.528, f32[4,640]{1,0:T(4,128)} %fusion.529, f32[4]{0:T(128)} %get-tuple-element.3373, pred[640,1280]{1,0:T(8,128)(4,1)S(1)} %get-tuple-element.3355, f32[4]{0:T(128)} %get-tuple-element.3374, ...), kind=kOutput, calls=%fused_computation.497.clone.3.clone | convolution fusion | flops 648803840 | bytes 54268432 | tf_op jit(solution)/shard_map/while/body/eval_jaxpr/qhd,khd->hqk/dot_general | solution.py:53
  1842.8 48.4 %fusion.533 = (f32[4]{0:T(128)S(1)}, f32[4]{0:T(128)}, f32[4]{0:T(128)}, f32[4]{0:T(128)}, f32[4]{0:T(128)}, /*index=5*/f32[4]{0:T(128)}, f32[4]{0:T(128)}, f32[...) fusion(pred[640,1280]{1,0:T(8,128)(4,1)S(1)} %get-tuple-element, ...), kind=kLoop, calls=%fused_computation.495.clone.1.clone | loop fusion | flops 131071968 | bytes 47524128 | tf_op jit(solution)/shard_map/while/body/eval_jaxpr/reduce_sum | solution.py:261
  1902.2 26.4 %fusion.537 = (f32[4]{0:T(128)S(1)}, f32[4]{0:T(128)S(1)}, f32[4]{0:T(128)S(1)}, f32[4]{0:T(128)S(1)}, f32[4]{0:T(128)S(1)}, /*index=5*/f32[4]{0:T(128)S(1)}, f3...) fusion(bf16[4,640,1280]{2,1,0:T(8,128)(2,1)S(1)} %get-tuple-ele, ...), kind=kLoop, calls=%fused_computation.494.clone.1.clone | loop fusion | flops 95027152 | bytes 18022624 | tf_op jit(solution)/shard_map/while/body/eval_jaxpr/reduce_sum | solution.py:261
  1969.0 23.6 %convolution_convert_fusion.1 = bf16[4096,1024]{1,0:T(8,128)(2,1)} fusion(bf16[1280,1024]{1,0:T(8,128)(2,1)} %param.35, f32[1280,4096]{1,0:T(8,128)} %fusion.356, f32[4096]{0:T(1024)S(1)} %bitcast.949), kind=kOutput, calls=%fused_computation.682 | convolution fusion | flops 10794041344 | bytes 31997952 | tf_op jit(solution)/shard_map/tf,td->fd/dot_general | solution.py:205
  1993.3 19.2 convolution_convert_fusion.2
  2039.5 22.1 add_convert_fusion.3
  2061.6 62.0 %reduce-scatter.12.cloned.1.call-done = bf16[512,1024]{1,0:T(8,128)(2,1)} async-done(((bf16[4096,1024]{1,0:T(8,128)(2,1)}), bf16[512,1024]{1,0:T(8,128)(2,1)}) %reduce-scatter.12.cloned.1.call-update) | async-done | bytes 1048592 | tf_op jit(solution)/shard_map/reduce_scatter | solution.py:323
  2123.6 75.2 %reduce-scatter.10.cloned.1.call-done = bf16[128,4096]{1,0:T(8,128)(2,1)} async-done(((bf16[1024,4096]{1,0:T(8,128)(2,1)}), bf16[128,4096]{1,0:T(8,128)(2,1)}) %reduce-scatter.10.cloned.1.call-update) | async-done | bytes 1048592 | tf_op jit(solution)/shard_map/reduce_scatter | solution.py:317
  2216.4 24.3 %all-reduce.9 = (bf16[32,16]{0,1:T(8,128)(2,1)S(1)}, bf16[1024]{0:T(1024)(128)(2,1)S(1)}, bf16[1024]{0:T(1024)(128)(2,1)S(1)}, bf16[1024]{0:T(1024)(128)(2,1)S(1...) all-reduce(bf16[32,16]{0,1:T(8,128)(2,1)S(1)} %bitcast.951, ...), channel_id=5, replica_groups=mesh['rep'=4,'fsdp'=8] {'fsdp'}, use_global_device_ids=true, to_apply=%region_96.97.clone | all-reduce | flops 9728 | bytes 38912
  2269.5 54.5 %all-reduce.14.cloned.1.call-done = (bf16[128,3072]{1,0:T(8,128)(2,1)}, bf16[128,1024]{1,0:T(8,128)(2,1)}, bf16[128,4096]{1,0:T(8,128)(2,1)}, bf16[512,1024]{1,0:T(8,128)(2,1)}) async-done(((bf16[128,3072]{1,0:T(8,128)(2,1)}, bf16[128,1024]{1,0:T(8,128)(2,1)}, bf16[128,4096]{1,0:T(8,128)(2,1)}, bf16[512,1024]{1,0:T(8,128)(2,1)}), (bf16[128,3072]{1,0:T(8,128)(2,1)}, bf16[128,1024]{1,0:T(8,128)(2,1)}, ...) | async-done | bytes 3145744 | tf_op jit(solution)/shard_map/psum | solution.py:346
  (1152 shorter events, 745.6 us)
Async XLA Ops:
  7.2 86.6 %all-gather.12.cloned.1.call-start = ((), (), s32[]{:S(2)}) async-start(), calls=%async_computation.4 | async-start | bytes 7077888 | tf_op jit(solution)/shard_map/all_gather | solution.py:91
  7.9 682.7 %all-gather.14.cloned.1.call-start = ((), (), s32[]{:S(2)}) async-start(), calls=%async_computation.5 | async-start | bytes 2359296 | tf_op jit(solution)/shard_map/all_gather | solution.py:93
  8.7 691.6 %all-gather.16.cloned.1.call-start = ((), (), s32[]{:S(2)}) async-start(), calls=%async_computation.6 | async-start | bytes 9437184 | tf_op jit(solution)/shard_map/all_gather | solution.py:96
  9.5 710.7 %all-gather.18.cloned.1.call-start = ((), (), s32[]{:S(2)}) async-start(), calls=%async_computation.7 | async-start | bytes 9437184 | tf_op jit(solution)/shard_map/all_gather | solution.py:98
  10.0 2051.5 %reduce-scatter.8.cloned.1.call-start = ((), (), s32[]{:S(2)}) async-start(), calls=%async_computation.9 | async-start | bytes 2359296 | tf_op jit(solution)/shard_map/reduce_scatter | solution.py:308
  24.0 69.8 %copy-start.83 = (f32[8,1,128]{2,1,0:T(1,128)}, f32[8,1,128]{2,1,0:T(1,128)S(1)}, u32[]{:S(2)}) copy-start(f32[8,1,128]{2,1,0:T(1,128)S(1)} %convert_element_type.12316) | copy-start | bytes 12292
  131.9 374.0 %copy-start.50 = (s32[640]{0:T(1024)S(1)}, s32[640]{0:T(1024)}, u32[]{:S(2)}) copy-start(s32[640]{0:T(1024)} %copy-done.49) | copy-start | bytes 7684
  131.9 374.0 %copy-start.51 = (s32[640]{0:T(1024)S(1)}, s32[640]{0:T(1024)}, u32[]{:S(2)}) copy-start(s32[640]{0:T(1024)} %get-tuple-element.3622) | copy-start | bytes 7684
  697.2 81.0 %copy-start.73 = (f32[1280]{0:T(1024)}, f32[1280]{0:T(1024)S(1)}, u32[]{:S(2)}) copy-start(f32[1280]{0:T(1024)S(1)} %broadcast_multiply_fusion) | copy-start | bytes 15364
  700.2 78.0 %copy-start.75 = (f32[1280]{0:T(1024)}, f32[1280]{0:T(1024)S(1)}, u32[]{:S(2)}) copy-start(f32[1280]{0:T(1024)S(1)} %fusion.349) | copy-start | bytes 15364
  794.4 351.1 %copy-start.58 = (s32[1280]{0:T(1024)S(1)}, s32[1280]{0:T(1024)}, u32[]{:S(2)}) copy-start(s32[1280]{0:T(1024)} %copy-done.57) | copy-start | bytes 15364
  794.5 351.1 %copy-start.64 = (s32[640]{0:T(1024)S(1)}, s32[640]{0:T(1024)}, u32[]{:S(2)}) copy-start(s32[640]{0:T(1024)} %copy-done.63) | copy-start | bytes 7684
  794.5 351.1 %copy-start.69 = (s32[640]{0:T(1024)S(1)}, s32[640]{0:T(1024)}, u32[]{:S(2)}) copy-start(s32[640]{0:T(1024)} %copy-done.68) | copy-start | bytes 7684
  1193.6 64.8 %copy-start.9 = (pred[640,1280]{1,0:T(8,128)(4,1)}, pred[640,1280]{1,0:T(8,128)(4,1)S(1)}, u32[]{:S(2)}) copy-start(pred[640,1280]{1,0:T(8,128)(4,1)S(1)} %get-tuple-element.3367) | copy-start | bytes 2457604 | tf_op jit(solution)/shard_map/while
  1193.6 64.8 %copy-start.10 = (pred[640,1280]{1,0:T(8,128)(4,1)}, pred[640,1280]{1,0:T(8,128)(4,1)S(1)}, u32[]{:S(2)}) copy-start(pred[640,1280]{1,0:T(8,128)(4,1)S(1)} %get-tuple-element.3366) | copy-start | bytes 2457604 | tf_op jit(solution)/shard_map/while
  1193.6 64.8 %copy-start.11 = (pred[640,1280]{1,0:T(8,128)(4,1)}, pred[640,1280]{1,0:T(8,128)(4,1)S(1)}, u32[]{:S(2)}) copy-start(pred[640,1280]{1,0:T(8,128)(4,1)S(1)} %get-tuple-element.3365) | copy-start | bytes 2457604 | tf_op jit(solution)/shard_map/while
  1193.6 64.8 %copy-start.12 = (pred[640,1280]{1,0:T(8,128)(4,1)}, pred[640,1280]{1,0:T(8,128)(4,1)S(1)}, u32[]{:S(2)}) copy-start(pred[640,1280]{1,0:T(8,128)(4,1)S(1)} %get-tuple-element.3364) | copy-start | bytes 2457604 | tf_op jit(solution)/shard_map/while
  1193.6 64.8 %copy-start.13 = (pred[640,1280]{1,0:T(8,128)(4,1)}, pred[640,1280]{1,0:T(8,128)(4,1)S(1)}, u32[]{:S(2)}) copy-start(pred[640,1280]{1,0:T(8,128)(4,1)S(1)} %get-tuple-element.3363) | copy-start | bytes 2457604 | tf_op jit(solution)/shard_map/while
  1193.7 64.8 %copy-start.14 = (pred[640,1280]{1,0:T(8,128)(4,1)}, pred[640,1280]{1,0:T(8,128)(4,1)S(1)}, u32[]{:S(2)}) copy-start(pred[640,1280]{1,0:T(8,128)(4,1)S(1)} %get-tuple-element.3362) | copy-start | bytes 2457604 | tf_op jit(solution)/shard_map/while
  1193.7 64.8 %copy-start.15 = (pred[640,1280]{1,0:T(8,128)(4,1)}, pred[640,1280]{1,0:T(8,128)(4,1)S(1)}, u32[]{:S(2)}) copy-start(pred[640,1280]{1,0:T(8,128)(4,1)S(1)} %get-tuple-element.3361) | copy-start | bytes 2457604 | tf_op jit(solution)/shard_map/while
  1193.7 64.8 %copy-start.16 = (pred[640,1280]{1,0:T(8,128)(4,1)}, pred[640,1280]{1,0:T(8,128)(4,1)S(1)}, u32[]{:S(2)}) copy-start(pred[640,1280]{1,0:T(8,128)(4,1)S(1)} %get-tuple-element.3360) | copy-start | bytes 2457604 | tf_op jit(solution)/shard_map/while
  1388.3 64.8 %copy-start.9 = (pred[640,1280]{1,0:T(8,128)(4,1)}, pred[640,1280]{1,0:T(8,128)(4,1)S(1)}, u32[]{:S(2)}) copy-start(pred[640,1280]{1,0:T(8,128)(4,1)S(1)} %get-tuple-element.3367) | copy-start | bytes 2457604 | tf_op jit(solution)/shard_map/while
  1388.4 64.8 %copy-start.10 = (pred[640,1280]{1,0:T(8,128)(4,1)}, pred[640,1280]{1,0:T(8,128)(4,1)S(1)}, u32[]{:S(2)}) copy-start(pred[640,1280]{1,0:T(8,128)(4,1)S(1)} %get-tuple-element.3366) | copy-start | bytes 2457604 | tf_op jit(solution)/shard_map/while
  1388.4 64.8 %copy-start.11 = (pred[640,1280]{1,0:T(8,128)(4,1)}, pred[640,1280]{1,0:T(8,128)(4,1)S(1)}, u32[]{:S(2)}) copy-start(pred[640,1280]{1,0:T(8,128)(4,1)S(1)} %get-tuple-element.3365) | copy-start | bytes 2457604 | tf_op jit(solution)/shard_map/while
  1388.4 64.8 %copy-start.12 = (pred[640,1280]{1,0:T(8,128)(4,1)}, pred[640,1280]{1,0:T(8,128)(4,1)S(1)}, u32[]{:S(2)}) copy-start(pred[640,1280]{1,0:T(8,128)(4,1)S(1)} %get-tuple-element.3364) | copy-start | bytes 2457604 | tf_op jit(solution)/shard_map/while
  1388.4 64.8 %copy-start.13 = (pred[640,1280]{1,0:T(8,128)(4,1)}, pred[640,1280]{1,0:T(8,128)(4,1)S(1)}, u32[]{:S(2)}) copy-start(pred[640,1280]{1,0:T(8,128)(4,1)S(1)} %get-tuple-element.3363) | copy-start | bytes 2457604 | tf_op jit(solution)/shard_map/while
  1583.1 64.8 %copy-start.9 = (pred[640,1280]{1,0:T(8,128)(4,1)}, pred[640,1280]{1,0:T(8,128)(4,1)S(1)}, u32[]{:S(2)}) copy-start(pred[640,1280]{1,0:T(8,128)(4,1)S(1)} %get-tuple-element.3367) | copy-start | bytes 2457604 | tf_op jit(solution)/shard_map/while
  1583.1 64.8 %copy-start.10 = (pred[640,1280]{1,0:T(8,128)(4,1)}, pred[640,1280]{1,0:T(8,128)(4,1)S(1)}, u32[]{:S(2)}) copy-start(pred[640,1280]{1,0:T(8,128)(4,1)S(1)} %get-tuple-element.3366) | copy-start | bytes 2457604 | tf_op jit(solution)/shard_map/while
  1583.1 64.8 %copy-start.11 = (pred[640,1280]{1,0:T(8,128)(4,1)}, pred[640,1280]{1,0:T(8,128)(4,1)S(1)}, u32[]{:S(2)}) copy-start(pred[640,1280]{1,0:T(8,128)(4,1)S(1)} %get-tuple-element.3365) | copy-start | bytes 2457604 | tf_op jit(solution)/shard_map/while
  1583.1 64.8 %copy-start.12 = (pred[640,1280]{1,0:T(8,128)(4,1)}, pred[640,1280]{1,0:T(8,128)(4,1)S(1)}, u32[]{:S(2)}) copy-start(pred[640,1280]{1,0:T(8,128)(4,1)S(1)} %get-tuple-element.3364) | copy-start | bytes 2457604 | tf_op jit(solution)/shard_map/while
  1583.1 64.8 %copy-start.13 = (pred[640,1280]{1,0:T(8,128)(4,1)}, pred[640,1280]{1,0:T(8,128)(4,1)S(1)}, u32[]{:S(2)}) copy-start(pred[640,1280]{1,0:T(8,128)(4,1)S(1)} %get-tuple-element.3363) | copy-start | bytes 2457604 | tf_op jit(solution)/shard_map/while
  1583.2 64.8 %copy-start.14 = (pred[640,1280]{1,0:T(8,128)(4,1)}, pred[640,1280]{1,0:T(8,128)(4,1)S(1)}, u32[]{:S(2)}) copy-start(pred[640,1280]{1,0:T(8,128)(4,1)S(1)} %get-tuple-element.3362) | copy-start | bytes 2457604 | tf_op jit(solution)/shard_map/while
  1583.2 64.8 %copy-start.15 = (pred[640,1280]{1,0:T(8,128)(4,1)}, pred[640,1280]{1,0:T(8,128)(4,1)S(1)}, u32[]{:S(2)}) copy-start(pred[640,1280]{1,0:T(8,128)(4,1)S(1)} %get-tuple-element.3361) | copy-start | bytes 2457604 | tf_op jit(solution)/shard_map/while
  1583.2 64.8 %copy-start.16 = (pred[640,1280]{1,0:T(8,128)(4,1)}, pred[640,1280]{1,0:T(8,128)(4,1)S(1)}, u32[]{:S(2)}) copy-start(pred[640,1280]{1,0:T(8,128)(4,1)S(1)} %get-tuple-element.3360) | copy-start | bytes 2457604 | tf_op jit(solution)/shard_map/while
  1777.9 64.8 %copy-start.9 = (pred[640,1280]{1,0:T(8,128)(4,1)}, pred[640,1280]{1,0:T(8,128)(4,1)S(1)}, u32[]{:S(2)}) copy-start(pred[640,1280]{1,0:T(8,128)(4,1)S(1)} %get-tuple-element.3367) | copy-start | bytes 2457604 | tf_op jit(solution)/shard_map/while
  1777.9 64.8 %copy-start.10 = (pred[640,1280]{1,0:T(8,128)(4,1)}, pred[640,1280]{1,0:T(8,128)(4,1)S(1)}, u32[]{:S(2)}) copy-start(pred[640,1280]{1,0:T(8,128)(4,1)S(1)} %get-tuple-element.3366) | copy-start | bytes 2457604 | tf_op jit(solution)/shard_map/while
  1777.9 64.8 %copy-start.11 = (pred[640,1280]{1,0:T(8,128)(4,1)}, pred[640,1280]{1,0:T(8,128)(4,1)S(1)}, u32[]{:S(2)}) copy-start(pred[640,1280]{1,0:T(8,128)(4,1)S(1)} %get-tuple-element.3365) | copy-start | bytes 2457604 | tf_op jit(solution)/shard_map/while
  1777.9 64.8 %copy-start.12 = (pred[640,1280]{1,0:T(8,128)(4,1)}, pred[640,1280]{1,0:T(8,128)(4,1)S(1)}, u32[]{:S(2)}) copy-start(pred[640,1280]{1,0:T(8,128)(4,1)S(1)} %get-tuple-element.3364) | copy-start | bytes 2457604 | tf_op jit(solution)/shard_map/while
  1777.9 64.8 %copy-start.13 = (pred[640,1280]{1,0:T(8,128)(4,1)}, pred[640,1280]{1,0:T(8,128)(4,1)S(1)}, u32[]{:S(2)}) copy-start(pred[640,1280]{1,0:T(8,128)(4,1)S(1)} %get-tuple-element.3363) | copy-start | bytes 2457604 | tf_op jit(solution)/shard_map/while
  1777.9 64.8 %copy-start.14 = (pred[640,1280]{1,0:T(8,128)(4,1)}, pred[640,1280]{1,0:T(8,128)(4,1)S(1)}, u32[]{:S(2)}) copy-start(pred[640,1280]{1,0:T(8,128)(4,1)S(1)} %get-tuple-element.3362) | copy-start | bytes 2457604 | tf_op jit(solution)/shard_map/while
  1777.9 64.8 %copy-start.15 = (pred[640,1280]{1,0:T(8,128)(4,1)}, pred[640,1280]{1,0:T(8,128)(4,1)S(1)}, u32[]{:S(2)}) copy-start(pred[640,1280]{1,0:T(8,128)(4,1)S(1)} %get-tuple-element.3361) | copy-start | bytes 2457604 | tf_op jit(solution)/shard_map/while
  1777.9 64.8 %copy-start.16 = (pred[640,1280]{1,0:T(8,128)(4,1)}, pred[640,1280]{1,0:T(8,128)(4,1)S(1)}, u32[]{:S(2)}) copy-start(pred[640,1280]{1,0:T(8,128)(4,1)S(1)} %get-tuple-element.3360) | copy-start | bytes 2457604 | tf_op jit(solution)/shard_map/while
  1942.0 119.5 %reduce-scatter.6.cloned.1.call-start = ((), (), s32[]{:S(2)}) async-start(), calls=%async_computation.8 | async-start | bytes 7077888 | tf_op jit(solution)/shard_map/reduce_scatter | solution.py:302
  1968.3 155.3 %reduce-scatter.12.cloned.1.call-start = ((), (), s32[]{:S(2)}) async-start(), calls=%async_computation.11 | async-start | bytes 9437184 | tf_op jit(solution)/shard_map/reduce_scatter | solution.py:323
  1992.6 206.2 %reduce-scatter.10.cloned.1.call-start = ((), (), s32[]{:S(2)}) async-start(), calls=%async_computation.10 | async-start | bytes 9437184 | tf_op jit(solution)/shard_map/reduce_scatter | solution.py:317
  2012.5 311.5 %all-reduce.14.cloned.1.call-start = ((), (), s32[]{:S(2)}) async-start(), calls=%async_computation.12 | async-start | bytes 6291456 | tf_op jit(solution)/shard_map/psum | solution.py:346
  2039.5 159.3 %copy-start.103 = (f32[4,32,4]{1,2,0:T(4,128)S(1)}, f32[4,32,4]{1,2,0:T(4,128)}, u32[]{:S(2)}) copy-start(f32[4,32,4]{1,2,0:T(4,128)} %get-tuple-element.3742) | copy-start | bytes 6148
  2039.5 159.3 %copy-start.105 = (f32[4,32,4]{1,2,0:T(4,128)S(1)}, f32[4,32,4]{1,2,0:T(4,128)}, u32[]{:S(2)}) copy-start(f32[4,32,4]{1,2,0:T(4,128)} %copy-done.104) | copy-start | bytes 6148
  (276 other events, 3979.1 us)
Sparse Core Ops, SparseCore 0:
  9.9 48.2 all-gather.11
  60.1 27.8 all-gather.13
  89.9 54.3 all-gather.15
  146.1 54.3 all-gather.17
  1942.1 41.2 reduce-scatter.7
  1987.0 61.7 reduce-scatter.5
  2052.3 71.2 reduce-scatter.11
  2127.4 71.2 reduce-scatter.9
  2201.4 122.5 all-reduce.13
where the time goes:
time: 2350 us; the launch traced here: 2340 us
  matrix products  1100 us (47%)
  other arithmetic  778 us (33%)
  waiting for transfers between devices  194 us (8%)
  local copies, waits for them, and re-layouts  126 us (5%)
  blocking collectives  96.5 us (4%)
    dot_general x16, matrix products, block_scores(): jnp.einsum('qhd,khd->hqk', query_rows, key_rows, preferred_element_type=j...  723 us
    reduce_sum x16, other arithmetic, attend_back(): jnp.sum(jnp.where(bucket[None] == bucket_id, grad_float, 0.0), axis=(1, 2))  426 us
    eq x16, other arithmetic, block_scores(): bucket[None] == bucket_id  234 us
    reduce_scatter x1, waiting for transfers between devices, local(): lax.psum_scatter(grad_w_up.astype(jnp.bfloat16), 'fsdp', scatter_dimensio...  75.2 us
    reduce_scatter x1, waiting for transfers between devices, local(): lax.psum_scatter(grad_w_down.astype(jnp.bfloat16), 'fsdp', scatter_dimens...  62 us
    psum x1, waiting for transfers between devices, local(): lax.psum(share_qkv.astype(jnp.bfloat16), 'rep').astype(jnp.float32)  54.5 us
    dot_general x8, matrix products, attend_back(): jnp.einsum('hqk,qhd->khd', probs.astype(jnp.bfloat16), grad_rows, preferr...  50.4 us
  transfers between devices with their start and end apart: 9, of which 3 were waited for; matrix products, arithmetic and copies ran while one was open for 34% of the time, Pallas kernels for 0%

commit v1 on v0

v1 whole, which is shorter than its diff:
```python
import jax
import jax.numpy as jnp
import numpy as np
from jax import lax
from jax.experimental import pallas as pl
from jax.experimental.pallas import tpu as pltpu
from jax.sharding import PartitionSpec as P

D = 1024
H = 16
HD = 64
NBUCKET = 32
MAXDIST = 128
bf16=jnp.bfloat16; f32=jnp.float32
NEG=-1e9
LONG=1024; SHORT=256; T=1280
NN=(((1,),(0,)),((),())); NT=(((1,),(1,)),((),())); TN=(((0,),(0,)),((),()))
def dot(a,b,dims): return lax.dot_general(a,b,dims,preferred_element_type=f32)
def split3(x):
    a=x.astype(bf16); r=x-a.astype(f32); b=r.astype(bf16); c=(r-b.astype(f32)).astype(bf16)
    return a,b,c

def fwd_body(bnd_ref,g_ref,q_ref,k_ref,v_ref,o_ref,qa_ref):
    lane=lax.broadcasted_iota(jnp.int32,(1,128),1)
    bnd=bnd_ref[0]
    r1=lax.broadcasted_iota(jnp.int32,(128,256),0); c1=lax.broadcasted_iota(jnp.int32,(128,256),1)
    outs=[]
    for h in range(2):
        mine=(lane<64) if h==0 else (lane>=64)
        base=64 if h==0 else 0
        g=g_ref[0,h:h+1,:]
        band=pltpu.roll(jnp.broadcast_to(g,(128,256)),0,1,stride=1,stride_axis=0)
        band=jnp.where(c1-128>r1,NEG,band)
        parts=[]; qas=[]
        for blk in range(5):
            R=256*blk
            lo=0 if blk<4 else 1024
            qrow=q_ref[R:R+256,:]*bf16(0.125)
            qm=jnp.where(mine,qrow,bf16(0))
            s=dot(qm,k_ref[lo:R+256,:],NT)
            nk=R+256-lo
            pieces=[]
            for sub in range(2):
                e=nk-256+128*(sub+1)
                rows=s[128*sub:128*sub+128]
                def mask(x,c0):
                    if blk<4: return x
                    rr=lax.broadcasted_iota(jnp.int32,x.shape,0)+128*sub
                    cc=lax.broadcasted_iota(jnp.int32,x.shape,1)+c0
                    return jnp.where((rr>=bnd)&(cc<bnd),NEG,x)
                segs=[]
                if e>=256:
                    if e>256: segs.append(rows[:,:e-256])
                    segs.append(mask(rows[:,e-256:e]+band,e-256))
                else:
                    segs.append(mask(rows[:,:128]+band[:,128:],0))
                m=None
                for sg in segs:
                    for c in range(0,sg.shape[1],128):
                        t=sg[:,c:c+128]
                        m=t if m is None else jnp.maximum(m,t)
                m=jnp.max(m,axis=1,keepdims=True)
                ps=[jnp.exp(sg-m).astype(bf16) for sg in segs]
                if e<nk: ps.append(jnp.zeros((128,nk-e),bf16))
                pieces.append((jnp.concatenate(ps,axis=1) if len(ps)>1 else ps[0],m))
            p=jnp.concatenate([pieces[0][0],pieces[1][0]],axis=0)
            m=jnp.concatenate([pieces[0][1],pieces[1][1]],axis=0)
            va=jnp.where(mine,v_ref[lo:R+256,:],jnp.where(lane==base,bf16(1),bf16(0)))
            o=dot(p,va,NN)
            l=o[:,base:base+1]
            parts.append(o*(1.0/l))
            a,b,c=split3(m+jnp.log(l))
            qas.append(jnp.where(mine,qrow,jnp.where(lane==base,a,jnp.where(lane==base+1,b,jnp.where(lane==base+2,c,bf16(0))))))
        for blk in range(5): qa_ref[256*blk:256*blk+256,128*h:128*h+128]=qas[blk]
        outs.append(parts)
    for blk in range(5):
        o_ref[256*blk:256*blk+256,:]=jnp.where(lane<64,outs[0][blk],outs[1][blk]).astype(bf16)

def attn_fwd(packed,g,bnd):
    return pl.pallas_call(fwd_body,
        grid=(8,),
        in_specs=[pl.BlockSpec(memory_space=pltpu.SMEM),
                  pl.BlockSpec((1,2,256),lambda i:(i,0,0)),
                  pl.BlockSpec((T,128),lambda i:(0,i)),
                  pl.BlockSpec((T,128),lambda i:(0,8+i)),
                  pl.BlockSpec((T,128),lambda i:(0,16+i))],
        out_specs=[pl.BlockSpec((T,128),lambda i:(0,i)),pl.BlockSpec((T,256),lambda i:(0,i))],
        out_shape=[jax.ShapeDtypeStruct((T,1024),bf16),jax.ShapeDtypeStruct((T,2048),bf16)],
        cost_estimate=pl.CostEstimate(flops=2*16*11*65536*128,bytes_accessed=16<<20,transcendentals=16*11*65536),
        compiler_params=pltpu.CompilerParams(vmem_limit_bytes=48<<20))(bnd,g,packed,packed,packed)

def bwd_body(bnd_ref,g_ref,qa_ref,k_ref,v_ref,o_ref,do_ref,gq_ref,gk_ref,gv_ref,gs_ref,dq_acc,band_acc):
    lane=lax.broadcasted_iota(jnp.int32,(1,128),1)
    bnd=bnd_ref[0]
    r1=lax.broadcasted_iota(jnp.int32,(128,256),0); c1=lax.broadcasted_iota(jnp.int32,(128,256),1)
    prod=do_ref[...].astype(f32)*o_ref[...].astype(f32)
    ph=prod.astype(bf16); plo=(prod-ph.astype(f32)).astype(bf16)
    i0=lax.broadcasted_iota(jnp.int32,(128,128),0); j0=lax.broadcasted_iota(jnp.int32,(128,128),1)
    sw=jnp.where((i0<64)!=(j0<64),bf16(1),bf16(0))
    delta=-(dot(ph,sw,NN)+dot(plo,sw,NN))
    dh,dl,_=split3(delta)
    gks=[];gvs=[]
    for h in range(2):
        mine=(lane<64) if h==0 else (lane>=64)
        base=64 if h==0 else 0
        g=g_ref[0,h:h+1,:]
        band=pltpu.roll(jnp.broadcast_to(g,(128,256)),0,1,stride=1,stride_axis=0)
        band=jnp.where(c1<r1,NEG,band)
        dob=do_ref[...]
        doa=jnp.where(mine,dob,jnp.where(lane==base,dh,jnp.where(lane==base+1,dl,bf16(0))))
        gk=[];gv=[]
        for blk in (3,2,1,0,4):
            R=256*blk
            hi=1024 if blk<4 else 1280
            nq=hi-R
            neg=jnp.where((lane>=base)&(lane<base+3),bf16(-1),bf16(0))
            one=jnp.where((lane>=base)&(lane<base+2),bf16(1),bf16(0))
            ka=jnp.where(mine,k_ref[R:R+256,:],neg)
            va=jnp.where(mine,v_ref[R:R+256,:],one)
            qa=qa_ref[R:hi,128*h:128*h+128]
            do=doa[R:hi]
            st=dot(ka,qa,NT)
            dpt=dot(va,do,NT)
            pr=[];dr=[]
            for sub in range(2):
                b0=128*sub
                w=min(256,nq-b0)
                sb=st[b0:b0+128,b0:b0+w]+band[:,:w]
                if blk==4:
                    rr=lax.broadcasted_iota(jnp.int32,sb.shape,0)+b0
                    cc=lax.broadcasted_iota(jnp.int32,sb.shape,1)+b0
                    sb=jnp.where((cc>=bnd)&(rr<bnd),NEG,sb)
                pb=jnp.exp(sb)
                db=pb*dpt[b0:b0+128,b0:b0+w]
                if h==0 or True:
                    if blk==3 and sub==0: band_acc[...]=db
                    elif w==256: band_acc[...]+=db
                    else: band_acc[:,:w]+=db
                ps=[pb.astype(bf16)]; ds=[db.astype(bf16)]
                if sub==1:
                    ps.insert(0,jnp.zeros((128,128),bf16)); ds.insert(0,jnp.zeros((128,128),bf16))
                if b0+w<nq:
                    pf=jnp.exp(st[b0:b0+128,b0+w:])
                    df=pf*dpt[b0:b0+128,b0+w:]
                    ps.append(pf.astype(bf16)); ds.append(df.astype(bf16))
                pr.append(jnp.concatenate(ps,axis=1) if len(ps)>1 else ps[0])
                dr.append(jnp.concatenate(ds,axis=1) if len(ds)>1 else ds[0])
            p=jnp.concatenate(pr,axis=0); ds=jnp.concatenate(dr,axis=0)
            gvb=dot(p,do,NN); gkb=dot(ds,qa,NN)
            dqb=dot(ds,ka,TN)
            if blk in (3,2,1,0):
                dq_acc[h,R:R+256,:]=dqb[:256]
                if nq>256: dq_acc[h,R+256:hi,:]+=dqb[256:]
            else:
                dq_acc[h,R:hi,:]=dqb
            gk.append((R,gkb)); gv.append((R,gvb))
        gks.append(gk);gvs.append(gv)
        Y=band_acc[...]
        n=64
        while n>=1:
            Y=Y[:n]+pltpu.roll(Y[n:2*n],256-n,1)
            n//=2
        gs_ref[0,h:h+1,:]=Y
    for (R,a),(_,b) in zip(*gks): gk_ref[R:R+256,:]=jnp.where(lane<64,a,b).astype(bf16)
    for (R,a),(_,b) in zip(*gvs): gv_ref[R:R+256,:]=jnp.where(lane<64,a,b).astype(bf16)
    gq_ref[...]=(jnp.where(lane<64,dq_acc[0],dq_acc[1])*0.125).astype(bf16)

def attn_bwd(packed,qa,o,do,g,bnd):
    sp=lambda off: pl.BlockSpec((T,128),lambda i:(0,off+i))
    sh=jax.ShapeDtypeStruct((T,1024),bf16)
    return pl.pallas_call(bwd_body,
        grid=(8,),
        in_specs=[pl.BlockSpec(memory_space=pltpu.SMEM),
                  pl.BlockSpec((1,2,256),lambda i:(i,0,0)),
                  pl.BlockSpec((T,256),lambda i:(0,i)),sp(8),sp(16),sp(0),sp(0)],
        out_specs=[sp(0),sp(0),sp(0),pl.BlockSpec((1,2,256),lambda i:(i,0,0))],
        out_shape=[sh,sh,sh,jax.ShapeDtypeStruct((8,2,256),f32)],
        scratch_shapes=[pltpu.VMEM((2,T,128),f32),pltpu.VMEM((128,256),f32)],
        cost_estimate=pl.CostEstimate(flops=5*16*11*65536*128,bytes_accessed=24<<20,transcendentals=16*11*65536),
        compiler_params=pltpu.CompilerParams(vmem_limit_bytes=56<<20))(bnd,g,qa,packed,packed,o,do)


def bucket_edges(bucket_count, reach_max):
    exact_count = bucket_count // 2
    edge_list = list(range(1, exact_count + 1))
    distance = np.arange(exact_count, 64 * reach_max)
    level_of = exact_count + np.floor(
        np.log(distance / exact_count)
        / np.log(reach_max / exact_count)
        * (bucket_count - exact_count)
    ).astype(np.int64)
    for bucket_id in range(exact_count + 1, bucket_count):
        edge_list.append(int(distance[np.argmax(level_of >= bucket_id)]))
    return edge_list


EDGES = np.array(bucket_edges(NBUCKET, MAXDIST))
BUCKET = np.array([int(np.sum(n >= EDGES)) for n in range(256)])


def onehot_bucket(distance, live):
    hot = (np.arange(NBUCKET)[:, None] == BUCKET[distance][None, :]) & live[None, :]
    return hot.astype(np.float32)


def gelu_tanh(values):
    return jax.nn.gelu(values, approximate=True)


def norm_stats(values):
    mean = jnp.mean(values, axis=-1, keepdims=True)
    center = values - mean
    spread = jnp.mean(center * center, axis=-1, keepdims=True)
    return center * lax.rsqrt(spread + 1e-05), lax.rsqrt(spread + 1e-05)


def norm_back(xhat, rstd, scaled):
    return rstd * (
        scaled
        - jnp.mean(scaled, axis=-1, keepdims=True)
        - xhat * jnp.mean(scaled * xhat, axis=-1, keepdims=True)
    )


def local(
    tokens, item_lengths, attn_gain, attn_shift, w_qkv, rel_table, w_out,
    ffn_gain, ffn_shift, w_up, up_bias, w_down, down_bias, cotangent,
):
    gather = lambda a: lax.all_gather(a, "fsdp", axis=0, tiled=True)
    pieces = (attn_gain, attn_shift, ffn_gain, ffn_shift, down_bias, up_bias, rel_table.reshape(-1))
    small = jnp.concatenate(pieces).reshape(1, -1)
    small_full = gather(small)
    qkv_full = gather(w_qkv)
    out_full = gather(w_out)
    up_full = gather(w_up)
    down_full = gather(w_down)
    cuts = np.cumsum([0] + [piece.size for piece in pieces])
    ways = small_full.shape[0]
    part = lambda i: small_full[:, cuts[i] : cuts[i + 1]].reshape(-1).astype(jnp.float32)
    gain_one, shift_one, gain_two, shift_two, down_bias_full, up_bias_full = (
        part(i) for i in range(6)
    )
    table = part(6).reshape(NBUCKET, H)
    lens = item_lengths[0]
    first, second = lens[0], lens[1]
    long_first = first == LONG
    long_mid = second == LONG
    start = jnp.where(long_first, 0, jnp.where(long_mid, first, first + second))
    bound = jnp.where(long_first, second, jnp.where(long_mid, lens[2], first)).reshape(1)
    rotate = lambda a, by: jnp.roll(a, by, axis=0)
    tok = rotate(tokens, -start)
    cot = rotate(cotangent, -start)
    relative = table - table[NBUCKET - 1 :]
    reach = np.arange(256)
    fwd_hot = onehot_bucket(np.maximum(128 - reach, 0), reach <= 128)
    bwd_hot = onehot_bucket(reach, reach < 129)
    spread_of = lambda hot: jnp.dot(
        relative.T, hot, precision=lax.Precision.HIGHEST, preferred_element_type=jnp.float32
    ).reshape(8, 2, 256)
    bias_fwd, bias_bwd = spread_of(fwd_hot), spread_of(bwd_hot)

    hidden = tok.astype(jnp.float32)
    xhat_one, rstd_one = norm_stats(hidden)
    normed = (xhat_one * gain_one + shift_one).astype(jnp.bfloat16)
    packed = jnp.dot(normed, qkv_full, preferred_element_type=jnp.float32).astype(jnp.bfloat16)
    mixed, query_aug = attn_fwd(packed, bias_fwd, bound)
    middle = hidden + jnp.dot(mixed, out_full, preferred_element_type=jnp.float32)
    xhat_two, rstd_two = norm_stats(middle)
    normed_two = (xhat_two * gain_two + shift_two).astype(jnp.bfloat16)
    pre_act = (
        jnp.dot(normed_two, up_full, preferred_element_type=jnp.float32) + up_bias_full
    )
    activ = gelu_tanh(pre_act).astype(jnp.bfloat16)
    cot_float = cot.astype(jnp.float32)
    grad_w_down = jnp.einsum("tf,td->fd", activ, cot, preferred_element_type=jnp.float32)
    grad_down_bias = jnp.sum(cot_float, axis=0)
    scatter = lambda a: lax.psum_scatter(
        a.astype(jnp.bfloat16), "fsdp", scatter_dimension=0, tiled=True
    )
    share_down = scatter(grad_w_down)
    grad_activ = jnp.einsum("td,fd->tf", cot, down_full, preferred_element_type=jnp.float32)
    grad_pre = jax.vjp(gelu_tanh, pre_act)[1](grad_activ)[0].astype(jnp.bfloat16)
    grad_w_up = jnp.einsum("td,tf->df", normed_two, grad_pre, preferred_element_type=jnp.float32)
    share_up = scatter(grad_w_up)
    grad_up_bias = jnp.sum(grad_pre.astype(jnp.float32), axis=0)
    grad_normed_two = jnp.einsum("tf,df->td", grad_pre, up_full, preferred_element_type=jnp.float32)
    grad_ffn_gain = jnp.sum(grad_normed_two * xhat_two, axis=0)
    grad_ffn_shift = jnp.sum(grad_normed_two, axis=0)
    grad_middle = cot_float + norm_back(xhat_two, rstd_two, grad_normed_two * gain_two)
    grad_attended = grad_middle.astype(jnp.bfloat16)
    grad_w_out = jnp.einsum("td,te->de", mixed, grad_attended, preferred_element_type=jnp.float32)
    share_out = scatter(grad_w_out)
    grad_mixed = jnp.einsum(
        "te,de->td", grad_attended, out_full, preferred_element_type=jnp.float32
    ).astype(jnp.bfloat16)
    gq, gk, gv, grad_reach = attn_bwd(packed, query_aug, mixed, grad_mixed, bias_bwd, bound)
    grad_packed = jnp.concatenate([gq, gk, gv], axis=1)
    near_hot = onehot_bucket(reach, reach < EDGES[-1])
    grad_near = jnp.dot(
        near_hot, grad_reach.reshape(H, 256).T,
        precision=lax.Precision.HIGHEST, preferred_element_type=jnp.float32,
    )
    far = (np.arange(NBUCKET) == NBUCKET - 1).astype(np.float32)[:, None]
    grad_rel_table = grad_near - far * jnp.sum(grad_near, axis=0, keepdims=True)
    grad_w_qkv = jnp.einsum("td,te->de", normed, grad_packed, preferred_element_type=jnp.float32)
    share_qkv = scatter(grad_w_qkv)
    grad_normed = jnp.einsum("te,de->td", grad_packed, qkv_full, preferred_element_type=jnp.float32)
    grad_attn_gain = jnp.sum(grad_normed * xhat_one, axis=0)
    grad_attn_shift = jnp.sum(grad_normed, axis=0)
    grad_tokens = (
        grad_middle + norm_back(xhat_one, rstd_one, grad_normed * gain_one)
    ).astype(jnp.bfloat16)
    grad_tokens = rotate(grad_tokens, start)
    ffn_out = jnp.dot(activ, down_full, preferred_element_type=jnp.float32) + down_bias_full
    output = rotate((middle + ffn_out).astype(jnp.bfloat16), start)

    flat = lambda a: a.reshape(ways, -1)
    vectors = jnp.concatenate(
        [
            flat(grad_attn_gain), flat(grad_attn_shift), flat(grad_ffn_gain),
            flat(grad_ffn_shift), flat(grad_down_bias), flat(grad_up_bias), flat(grad_rel_table),
        ],
        axis=1,
    )
    share_small = lax.psum_scatter(
        vectors.astype(jnp.bfloat16), "fsdp", scatter_dimension=0, tiled=True
    )
    total = lambda a: lax.psum(a, "rep").astype(jnp.float32)
    sum_small = total(share_small)
    cut = lambda i: sum_small[0, cuts[i] : cuts[i + 1]]
    return (
        output, grad_tokens, cut(0), cut(1), total(share_qkv), cut(6).reshape(-1, H),
        total(share_out), cut(2), cut(3), total(share_up), cut(5), total(share_down), cut(4),
    )


def solution(mesh):
    rows, vec, mat = P(("rep", "fsdp"), None), P("fsdp"), P("fsdp", None)
    in_specs = (rows, rows, vec, vec, mat, mat, mat, vec, vec, mat, vec, mat, vec, rows)
    out_specs = (rows, rows, vec, vec, mat, mat, mat, vec, vec, mat, vec, mat, vec)
    return jax.shard_map(local, mesh=mesh, in_specs=in_specs, out_specs=out_specs, check_vma=False)
```

time: 2350 us -> 690 us (0.29)
  matrix products: 1100 us -> 192 us
  other arithmetic: 778 us -> 38.5 us
  local copies, waits for them, and re-layouts: 126 us -> 25.3 us
  Pallas kernels: 0 us -> 75.3 us
  waiting for transfers between devices: 194 us -> 266 us
  blocking collectives: 96.5 us -> 62 us
    dot_general x61 -> x8, matrix products: 1010 us -> 97.1 us  [the longest x1 30.1 us: local(): jnp.einsum('td,fd->tf', cot, down_full, preferred_element_type=jnp.float32)]
    reduce_sum x32 -> x3, other arithmetic: 478 us -> 3.68 us  [the longest x1 2.2 us: norm_stats(): mean = jnp.mean(values, axis=-1, keepdims=True)]
    eq x16 -> x0, other arithmetic: 234 us -> none  [block_scores(): bucket[None] == bucket_id]
    pallas_call x0 -> x2, Pallas kernels: none -> 75.3 us  [the longest x1 41.7 us: attn_bwd(): pl.pallas_call(bwd_body, grid=(8,), in_specs=[pl.BlockSpec(memory_space=p...]
    all_gather x4, waiting for transfers between devices: 0.06 us -> 60.2 us  [local(): gather = lambda a: lax.all_gather(a, 'fsdp', axis=0, tiled=True)]
    all_gather x7 -> x0, blocking collectives: 59.4 us -> none  [the longest x1 10.2 us: local(): lax.all_gather(attn_gain, 'fsdp', axis=0, tiled=True)]
    psum x1, waiting for transfers between devices: 54.5 us -> 95.6 us  [local(): total = lambda a: lax.psum(a, 'rep').astype(jnp.float32)]
    reduce_scatter x4, waiting for transfers between devices: 137 us -> 108 us  [local(): lax.psum_scatter(a.astype(jnp.bfloat16), 'fsdp', scatter_dimension=0, til...]
  transfers between devices with their start and end apart: 9 -> 9, of which waited for: 3 -> 5; matrix products, arithmetic and copies ran while one was open for 34% -> 26% of each run, Pallas kernels for 0% -> 11%
where the time goes in v1:
time: 690 us; the launch traced here: 681 us
  waiting for transfers between devices  266 us (39%)
  matrix products  192 us (28%)
  Pallas kernels  75.3 us (11%)
  blocking collectives  62 us (9%)
  other arithmetic  38.5 us (6%)
  local copies, waits for them, and re-layouts  25.3 us (4%)
  between operations  20.5 us (3%)
    reduce_scatter x4, waiting for transfers between devices, local(): lax.psum_scatter(a.astype(jnp.bfloat16), 'fsdp', scatter_dimension=0, til...  108 us
    psum x1, waiting for transfers between devices, local(): total = lambda a: lax.psum(a, 'rep').astype(jnp.float32)  95.6 us
    all_gather x4, waiting for transfers between devices, local(): gather = lambda a: lax.all_gather(a, 'fsdp', axis=0, tiled=True)  60.2 us
    unnamed x2, blocking collectives  50.1 us
    pallas_call x1, Pallas kernels, attn_bwd(): pl.pallas_call(bwd_body, grid=(8,), in_specs=[pl.BlockSpec(memory_space=p...  41.7 us
    pallas_call x1, Pallas kernels, attn_fwd(): pl.pallas_call(fwd_body, grid=(8,), in_specs=[pl.BlockSpec(memory_space=p...  33.6 us
    dot_general x1, matrix products, local(): jnp.einsum('td,fd->tf', cot, down_full, preferred_element_type=jnp.float32)  30.1 us
    dot_general x1, matrix products, local(): jnp.einsum('tf,td->fd', activ, cot, preferred_element_type=jnp.float32)  23.5 us
  transfers between devices with their start and end apart: 9, of which 5 were waited for; matrix products, arithmetic and copies ran while one was open for 26% of the time, Pallas kernels for 11%

profile of v1, /device:TPU:0, one launch (start us, length us, event | category | flops | bytes accessed | tf_op | source)
XLA Modules:
  0.0 680.8 jit_solution(8840184267612519583)
XLA Ops:
  8.0 0.7 all-gather.8.cloned.1.call-update
  10.0 1.4 fusion.48
  14.7 0.8 reshape.175
  17.4 1.3 fusion.47
  19.4 0.9 dynamic-update-slice.11
  20.2 0.8 dynamic-update-slice.12
  21.1 0.8 dynamic-update-slice.13
  21.9 0.8 dynamic-update-slice.14
  22.7 0.8 dynamic-update-slice.15
  23.6 0.9 dynamic-update-slice.16
  24.9 26.0 %all-reduce = bf16[9728]{0:T(1024)(128)(2,1)S(1)} all-reduce(bf16[9728]{0:T(1024)(128)(2,1)S(1)} %dynamic-update-slice), channel_id=2, replica_groups=mesh['rep'=4,'fsdp'=8] {'fsdp'}, use_global_device_ids=true, to_apply=%add | all-reduce | flops 9728 | bytes 38912
  51.3 0.9 fusion.29
  52.9 0.9 fusion.31
  53.8 5.8 fusion.43
  59.6 2.2 convert_reduce_fusion
  61.8 0.8 fusion.21
  63.3 13.7 %convolution_convert_fusion.q_ref.k_ref.v_ref = bf16[1280,3072]{1,0:T(8,128)(2,1)} fusion(bf16[1024,3072]{1,0:T(8,128)(2,1)} %all-gather.6.cloned.1.call-done, bf16[1280,1024]{1,0:T(8,128)(2,1)S(1)} %get-tuple-element.43, f32[1024]{0:T(1024)S(1)} %get-tuple-element.47, f32[1024]{0:T(1024)S(1)} %get-tuple-element.48, f32[1280]{0:T(1024)S(1)} %add_rsqrt_fusion.1, ...), kind=kOutput, calls=%fused_computation.10 | convolution fusion | flops 8064860160 | bytes 16795648 | tf_op jit(solution)/shard_map/dot_general | solution.py:265
  76.9 33.6 %shard_map.273 = (bf16[1280,1024]{1,0:T(8,128)(2,1)S(1)}, bf16[1280,2048]{1,0:T(8,128)(2,1)}) custom-call(s32[1]{0:T(128)} %bitcast.3.bnd_ref, f32[8,2,256]{2,1,0:T(2,128)S(1)} %copy.41.g_ref, bf16[1280,3072]{1,0:T(8,128)(2,1)} %convolution_convert_fusion.q_ref.k_ref.v_ref, bf16[1280,3072]{1,0:T(8,128)(2,1)} %convolution_convert_fusion.q_ref.k_ref.v_ref, ...), custom_call_target="tpu_custom_call" | custom-call | flops 2952790016 | bytes 16777216 | tf_op jit(solution)/shard_map/pallas_call | solution.py:80
  110.6 6.3 fusion.49
  116.9 3.1 copy-done.3
  120.7 23.7 %all-gather.10.cloned.1.call-done = bf16[1024,4096]{1,0:T(8,128)(2,1)} async-done(((bf16[128,4096]{1,0:T(8,128)(2,1)}), bf16[1024,4096]{1,0:T(8,128)(2,1)}) %all-gather.10.cloned.1.call-update) | async-done | bytes 8388624 | tf_op jit(solution)/shard_map/all_gather | solution.py:229
  144.4 19.7 %fusion.40 = f32[1280,4096]{1,0:T(8,128)} fusion(bf16[1024,4096]{1,0:T(8,128)(2,1)} %all-gather.10.cloned.1.call-done, f32[1280,1024]{1,0:T(8,128)} %copy-done.3, f32[1024]{0:T(1024)S(1)} %get-tuple-element.46, f32[1024]{0:T(1024)S(1)} %get-tuple-element.44, f32[1280]{0:T(1024)S(1)} %add_rsqrt_fusion, f32[1280]{0:T(1024)S(1)} %broadcast_multiply_fusion.4), kind=kOutput, calls=%fused_computation.102 | convolution fusion | flops 10743971840 | bytes 34621440 | tf_op jit(solution)/shard_map/dot_general | solution.py:271
  164.1 36.5 %all-gather.12.cloned.1.call-done = bf16[4096,1024]{1,0:T(8,128)(2,1)} async-done(((bf16[512,1024]{1,0:T(8,128)(2,1)}), bf16[4096,1024]{1,0:T(8,128)(2,1)}) %all-gather.12.cloned.1.call-update) | async-done | bytes 8388624 | tf_op jit(solution)/shard_map/all_gather | solution.py:229
  200.6 30.1 %fusion.41 = (bf16[4096]{0:T(1024)(128)(2,1)S(1)}, bf16[1280,4096]{1,0:T(8,128)(2,1)}) fusion(f32[1280,4096]{1,0:T(8,128)} %fusion.40, f32[4096]{0:T(1024)S(1)} %bitcast.86, bf16[1280,1024]{1,0:T(8,128)(2,1)} %get-tuple-element.41, bf16[4096,1024]{1,0:T(8,128)(2,1)} %all-gather.12.cloned.1.call-done), kind=kOutput, calls=%fused_computation.103 | convolution fusion | flops 10852757504 | bytes 42491904 | tf_op jit(solution)/shard_map/td,fd->tf/dot_general | solution.py:281
  230.7 18.8 %multiply_reduce_fusion = (bf16[1024]{0:T(1024)(128)(2,1)S(1)}, f32[1280]{0:T(1024)S(1)}, f32[1280]{0:T(1024)S(1)}, bf16[1024]{0:T(1024)(128)(2,1)S(1)}, f32[1280,1024]{1,0:T(8,128)}) fusion(f32[1280,1024]{1,0:T(8,128)S(1)} %copy-done.4, f32[1280]{0:T(1024)S(1)} %add_rsqrt_fusion, f32[1280]{0:T(1024)S(1)} %broadcast_multiply_fusion.4, ...), kind=kOutput, calls=%fused_computation.40 | convolution fusion | flops 10749210624 | bytes 29388800 | tf_op jit(solution)/shard_map/tf,df->td/dot_general | solution.py:286
  249.5 4.8 multiply_add_fusion
  254.3 2.2 copy-done.5
  256.5 4.2 convolution_convert_fusion.5
  260.7 7.6 %convolution_convert_fusion.4.do_ref = bf16[1280,1024]{1,0:T(8,128)(2,1)} fusion(bf16[1024,1024]{1,0:T(8,128)(2,1)} %all-gather.8.cloned.1.call-done, f32[1280,1024]{1,0:T(8,128)} %copy-done.5), kind=kOutput, calls=%fused_computation.49 | convolution fusion | flops 2686976000 | bytes 9961472 | tf_op jit(solution)/shard_map/te,de->td/dot_general | solution.py:293
  268.3 41.7 %shard_map.274 = (bf16[1280,1024]{1,0:T(8,128)(2,1)}, bf16[1280,1024]{1,0:T(8,128)(2,1)}, bf16[1280,1024]{1,0:T(8,128)(2,1)}, f32[8,2,256]{2,1,0:T(2,128)}) custom-call(s32[1]{0:T(128)} %bitcast.3.bnd_ref, f32[8,2,256]{2,1,0:T(2,128)} %copy.43.g_ref, bf16[1280,2048]{1,0:T(8,128)(2,1)} %get-tuple-element.21.qa_ref, ...), custom_call_target="tpu_custom_call" | custom-call | flops 7381975040 | bytes 25165824 | tf_op jit(solution)/shard_map/pallas_call | solution.py:171
  310.0 2.1 constant_dynamic-update-slice_fusion.2
  313.6 3.1 copy-done.12
  316.7 11.8 %convolution_convert_fusion.3 = bf16[1024,3072]{1,0:T(8,128)(2,1)} fusion(bf16[1280,3072]{1,0:T(8,128)(2,1)S(1)} %constant_dynamic-update-slice_fusion, bf16[1280,1024]{1,0:T(8,128)(2,1)S(1)} %copy-done.2, f32[1024]{0:T(1024)S(1)} %get-tuple-element.47, f32[1024]{0:T(1024)S(1)} %get-tuple-element.48, f32[1280]{0:T(1024)S(1)} %add_rsqrt_fusion.1, ...), kind=kOutput, calls=%fused_computation.22 | convolution fusion | flops 8064073728 | bytes 16795648 | tf_op jit(solution)/shard_map/td,te->de/dot_general | solution.py:305
  328.6 23.5 %convolution_convert_fusion.1 = bf16[4096,1024]{1,0:T(8,128)(2,1)} fusion(bf16[1280,1024]{1,0:T(8,128)(2,1)} %get-tuple-element.41, f32[1280,4096]{1,0:T(8,128)} %fusion.40, f32[4096]{0:T(1024)S(1)} %bitcast.87), kind=kOutput, calls=%fused_computation.14 | convolution fusion | flops 10794041344 | bytes 31997952 | tf_op jit(solution)/shard_map/tf,td->fd/dot_general | solution.py:275
  352.2 18.9 %convolution_convert_fusion.2 = bf16[1024,4096]{1,0:T(8,128)(2,1)} fusion(bf16[1280,4096]{1,0:T(8,128)(2,1)} %get-tuple-element.39, f32[1280,1024]{1,0:T(8,128)} %copy-done.3, f32[1024]{0:T(1024)S(1)} %get-tuple-element.46, f32[1024]{0:T(1024)S(1)} %get-tuple-element.44, f32[1280]{0:T(1024)S(1)} %add_rsqrt_fusion, f32[1280]{0:T(1024)S(1)} %broadcast_multiply_fusion.4), kind=kOutput, calls=%fused_computation.15 | convolution fusion | flops 10748166144 | bytes 24135680 | tf_op jit(solution)/shard_map/td,tf->df/dot_general | solution.py:283
  372.4 15.1 %fusion.20 = (bf16[1024]{0:T(1024)(128)(2,1)S(1)}, f32[1280]{0:T(1024)S(1)}, f32[1280]{0:T(1024)S(1)}, bf16[1024]{0:T(1024)(128)(2,1)S(1)}, f32[1280,1024]{1,0:T(8,128)}) fusion(bf16[1280,1024]{1,0:T(8,128)(2,1)S(1)} %copy-done.2, f32[1280]{0:T(1024)S(1)} %add_rsqrt_fusion.1, f32[1280]{0:T(1024)S(1)} %broadcast_multiply_fusion.5, ...), kind=kOutput, calls=%fused_computation.30 | convolution fusion | flops 8066166784 | bytes 22048768 | tf_op jit(solution)/shard_map/te,de->td/dot_general | solution.py:307
  387.6 24.1 %all-reduce.1 = bf16[8,1216]{1,0:T(8,128)(2,1)S(1)} all-reduce(bf16[8,1216]{1,0:T(8,128)(2,1)S(1)} %constant_dynamic-update-slice_fusion.3), channel_id=3, replica_groups=mesh['rep'=4,'fsdp'=8] {'fsdp'}, use_global_device_ids=true, to_apply=%region_15.17.clone | all-reduce | flops 9728 | bytes 38912
  412.3 11.8 %psum.35 = bf16[1,1216]{1,0:T(2,128)(2,1)S(1)} all-reduce(bf16[1,1216]{1,0:T(2,128)(2,1)S(1)} %constant_dynamic-slice_fusion), channel_id=1, replica_groups=mesh['rep'=4,'fsdp'=8] {'rep'}, use_global_device_ids=true, to_apply=%region_16.18 | all-reduce | flops 1216 | bytes 4864 | tf_op jit(solution)/shard_map/psum | solution.py:328
  426.0 6.6 fusion.19
  432.6 32.6 %reduce-scatter.11.cloned.1.call-done = bf16[512,1024]{1,0:T(8,128)(2,1)} async-done(((bf16[4096,1024]{1,0:T(8,128)(2,1)}), bf16[512,1024]{1,0:T(8,128)(2,1)}) %reduce-scatter.11.cloned.1.call-update) | async-done | bytes 1048592 | tf_op jit(solution)/shard_map/reduce_scatter | solution.py:277
  465.2 75.2 %reduce-scatter.9.cloned.1.call-done = bf16[128,4096]{1,0:T(8,128)(2,1)} async-done(((bf16[1024,4096]{1,0:T(8,128)(2,1)}), bf16[128,4096]{1,0:T(8,128)(2,1)}) %reduce-scatter.9.cloned.1.call-update) | async-done | bytes 1048592 | tf_op jit(solution)/shard_map/reduce_scatter | solution.py:277
  540.4 20.8 %add_convert_fusion = bf16[1280,1024]{1,0:T(8,128)(2,1)S(1)} fusion(f32[1280,1024]{1,0:T(8,128)} %copy-done.3, bf16[4096,1024]{1,0:T(8,128)(2,1)} %all-gather.12.cloned.1.call-done, f32[1024]{0:T(1024)S(1)} %copy-done.16, f32[1280,4096]{1,0:T(8,128)} %fusion.40, f32[4096]{0:T(1024)S(1)} %bitcast.88), kind=kOutput, calls=%fused_computation.43 | convolution fusion | flops 10793779200 | bytes 37244928 | tf_op jit(solution)/shard_map/dot_general | solution.py:314
  561.3 8.3 %fusion.22 = (bf16[1280,1024]{1,0:T(8,128)(2,1)}, bf16[1280,1024]{1,0:T(8,128)(2,1)}) fusion(s32[]{:T(128)S(6)} %select_n.36, bf16[1280,1024]{1,0:T(8,128)(2,1)S(1)} %copy-done.6, bf16[1280,1024]{1,0:T(8,128)(2,1)S(1)} %add_convert_fusion), kind=kLoop, calls=%fused_computation.50 | loop fusion | flops 10485760 | bytes 10485764 | tf_op jit(solution)/shard_map/jit(_roll_dynamic)/concatenate | solution.py:250
  569.6 95.6 %all-reduce.5.cloned.1.call-done = (bf16[128,3072]{1,0:T(8,128)(2,1)}, bf16[128,1024]{1,0:T(8,128)(2,1)}, bf16[128,4096]{1,0:T(8,128)(2,1)}, bf16[512,1024]{1,0:T(8,128)(2,1)}) async-done(((bf16[128,3072]{1,0:T(8,128)(2,1)}, bf16[128,1024]{1,0:T(8,128)(2,1)}, bf16[128,4096]{1,0:T(8,128)(2,1)}, bf16[512,1024]{1,0:T(8,128)(2,1)}), (bf16[128,3072]{1,0:T(8,128)(2,1)}, bf16[128,1024]{1,0:T(8,128)(2,1)}, ...) | async-done | bytes 3145744 | tf_op jit(solution)/shard_map/psum | solution.py:328
  665.1 1.9 convert_element_type.165
  667.0 2.4 convert_element_type.163
  669.5 2.8 convert_element_type.167
  672.2 1.6 convert_element_type.169
  (100 shorter events, 10.3 us)
Async XLA Ops:
  7.2 46.6 %copy-start.7 = (bf16[1280,1024]{1,0:T(8,128)(2,1)S(1)}, bf16[1280,1024]{1,0:T(8,128)(2,1)}, u32[]{:S(2)}) copy-start(bf16[1280,1024]{1,0:T(8,128)(2,1)} %param.33) | copy-start | bytes 7864324
  7.2 56.1 %all-gather.6.cloned.1.call-start = ((), (), s32[]{:S(2)}) async-start(), calls=%async_computation.4 | async-start | bytes 7077888 | tf_op jit(solution)/shard_map/all_gather | solution.py:229
  7.9 102.6 %all-gather.8.cloned.1.call-start = ((), (), s32[]{:S(2)}) async-start(), calls=%async_computation.5 | async-start | bytes 2359296 | tf_op jit(solution)/shard_map/all_gather | solution.py:229
  8.7 135.8 %all-gather.10.cloned.1.call-start = ((), (), s32[]{:S(2)}) async-start(), calls=%async_computation.6 | async-start | bytes 9437184 | tf_op jit(solution)/shard_map/all_gather | solution.py:229
  9.4 191.2 %all-gather.12.cloned.1.call-start = ((), (), s32[]{:S(2)}) async-start(), calls=%async_computation.7 | async-start | bytes 9437184 | tf_op jit(solution)/shard_map/all_gather | solution.py:229
  10.0 422.6 %reduce-scatter.7.cloned.1.call-start = ((), (), s32[]{:S(2)}) async-start(), calls=%async_computation.9 | async-start | bytes 2359296 | tf_op jit(solution)/shard_map/reduce_scatter | solution.py:277
  53.8 5.8 copy-start.10
  61.8 15.1 %copy-start.1 = (bf16[1280,1024]{1,0:T(8,128)(2,1)}, bf16[1280,1024]{1,0:T(8,128)(2,1)S(1)}, u32[]{:S(2)}) copy-start(bf16[1280,1024]{1,0:T(8,128)(2,1)S(1)} %get-tuple-element.43) | copy-start | bytes 7864324
  110.6 143.7 %copy-start = (bf16[1280,1024]{1,0:T(8,128)(2,1)}, bf16[1280,1024]{1,0:T(8,128)(2,1)S(1)}, u32[]{:S(2)}) copy-start(bf16[1280,1024]{1,0:T(8,128)(2,1)S(1)} %get-tuple-element.20.o_ref) | copy-start | bytes 7864324
  116.9 3.1 copy-start.3
  200.6 30.1 %copy-start.4 = (f32[1280,1024]{1,0:T(8,128)S(1)}, f32[1280,1024]{1,0:T(8,128)}, u32[]{:S(2)}) copy-start(f32[1280,1024]{1,0:T(8,128)} %copy-done.3) | copy-start | bytes 15728644
  254.2 2.2 copy-start.5
  260.7 171.9 %reduce-scatter.5.cloned.1.call-start = ((), (), s32[]{:S(2)}) async-start(), calls=%async_computation.8 | async-start | bytes 7077888 | tf_op jit(solution)/shard_map/reduce_scatter | solution.py:277
  310.0 2.5 copy-start.9
  310.0 3.3 copy-start.8
  312.5 4.2 copy-start.2
  313.6 3.1 copy-start.12
  328.5 136.7 %reduce-scatter.11.cloned.1.call-start = ((), (), s32[]{:S(2)}) async-start(), calls=%async_computation.11 | async-start | bytes 9437184 | tf_op jit(solution)/shard_map/reduce_scatter | solution.py:277
  352.1 188.2 %reduce-scatter.9.cloned.1.call-start = ((), (), s32[]{:S(2)}) async-start(), calls=%async_computation.10 | async-start | bytes 9437184 | tf_op jit(solution)/shard_map/reduce_scatter | solution.py:277
  371.1 0.7 copy-start.14
  371.1 0.8 copy-start.13
  371.1 1.0 copy-start.17
  371.1 294.0 %all-reduce.5.cloned.1.call-start = ((), (), s32[]{:S(2)}) async-start(), calls=%async_computation.12 | async-start | bytes 6291456 | tf_op jit(solution)/shard_map/psum | solution.py:328
  372.4 15.2 %copy-start.15 = (bf16[1024]{0:T(1024)(128)(2,1)S(1)}, bf16[1024]{0:T(1024)(128)(2,1)}, u32[]{:S(2)}) copy-start(bf16[1024]{0:T(1024)(128)(2,1)} %get-tuple-element.40) | copy-start | bytes 6148
  426.0 114.4 %copy-start.16 = (f32[1024]{0:T(1024)S(1)}, f32[1024]{0:T(1024)}, u32[]{:S(2)}) copy-start(f32[1024]{0:T(1024)} %get-tuple-element.45) | copy-start | bytes 12292
  540.4 20.9 %copy-start.6 = (bf16[1280,1024]{1,0:T(8,128)(2,1)S(1)}, bf16[1280,1024]{1,0:T(8,128)(2,1)}, u32[]{:S(2)}) copy-start(bf16[1280,1024]{1,0:T(8,128)(2,1)} %fusion.19) | copy-start | bytes 7864324
  665.1 7.1 %copy-start.11 = (bf16[512,1024]{1,0:T(8,128)(2,1)S(1)}, bf16[512,1024]{1,0:T(8,128)(2,1)}, u32[]{:S(2)}) copy-start(bf16[512,1024]{1,0:T(8,128)(2,1)} %get-tuple-element.37) | copy-start | bytes 3145732
Sparse Core Ops, SparseCore 0:
  9.9 48.4 all-gather.5
  60.3 27.7 all-gather.7
  90.0 54.3 all-gather.9
  146.2 54.3 all-gather.11
  260.8 41.1 reduce-scatter.6
  328.6 61.7 reduce-scatter.4
  393.9 71.2 reduce-scatter.10
  469.1 71.2 reduce-scatter.8
  543.0 122.0 all-reduce.4

commit v2 on v1

--- a/solution.py
+++ b/solution.py
@@ -1,3 +1,5 @@
+import functools
+
 import jax
 import jax.numpy as jnp
 import numpy as np
@@ -9,16 +11,30 @@
 D = 1024
 H = 16
 HD = 64
+FF = 4096
 NBUCKET = 32
 MAXDIST = 128
-bf16=jnp.bfloat16; f32=jnp.float32
-NEG=-1e9
-LONG=1024; SHORT=256; T=1280
-NN=(((1,),(0,)),((),())); NT=(((1,),(1,)),((),())); TN=(((0,),(0,)),((),()))
-def dot(a,b,dims): return lax.dot_general(a,b,dims,preferred_element_type=f32)
+bf16 = jnp.bfloat16
+f32 = jnp.float32
+NEG = -1e9
+LONG = 1024
+SHORT = 256
+T = 1280
+NN = (((1,), (0,)), ((), ()))
+NT = (((1,), (1,)), ((), ()))
+TN = (((0,), (0,)), ((), ()))
+
+
+def dot(a, b, dims):
+    return lax.dot_general(a, b, dims, preferred_element_type=f32)
+
+
 def split3(x):
-    a=x.astype(bf16); r=x-a.astype(f32); b=r.astype(bf16); c=(r-b.astype(f32)).astype(bf16)
-    return a,b,c
+    a = x.astype(bf16)
+    r = x - a.astype(f32)
+    b = r.astype(bf16)
+    return a, b, (r - b.astype(f32)).astype(bf16)
+
 
 def fwd_body(bnd_ref,g_ref,q_ref,k_ref,v_ref,o_ref,qa_ref):
     lane=lax.broadcasted_iota(jnp.int32,(1,128),1)
@@ -89,7 +105,7 @@
         cost_estimate=pl.CostEstimate(flops=2*16*11*65536*128,bytes_accessed=16<<20,transcendentals=16*11*65536),
         compiler_params=pltpu.CompilerParams(vmem_limit_bytes=48<<20))(bnd,g,packed,packed,packed)
 
-def bwd_body(bnd_ref,g_ref,qa_ref,k_ref,v_ref,o_ref,do_ref,gq_ref,gk_ref,gv_ref,gs_ref,dq_acc,band_acc):
+def bwd_body(bnd_ref,g_ref,qa_ref,k_ref,v_ref,o_ref,do_ref,grad_ref,gs_ref,dq_acc,band_acc):
     lane=lax.broadcasted_iota(jnp.int32,(1,128),1)
     bnd=bnd_ref[0]
     r1=lax.broadcasted_iota(jnp.int32,(128,256),0); c1=lax.broadcasted_iota(jnp.int32,(128,256),1)
@@ -161,23 +177,630 @@
             Y=Y[:n]+pltpu.roll(Y[n:2*n],256-n,1)
             n//=2
         gs_ref[0,h:h+1,:]=Y
-    for (R,a),(_,b) in zip(*gks): gk_ref[R:R+256,:]=jnp.where(lane<64,a,b).astype(bf16)
-    for (R,a),(_,b) in zip(*gvs): gv_ref[R:R+256,:]=jnp.where(lane<64,a,b).astype(bf16)
-    gq_ref[...]=(jnp.where(lane<64,dq_acc[0],dq_acc[1])*0.125).astype(bf16)
-
-def attn_bwd(packed,qa,o,do,g,bnd):
-    sp=lambda off: pl.BlockSpec((T,128),lambda i:(0,off+i))
-    sh=jax.ShapeDtypeStruct((T,1024),bf16)
+    for (R,a),(_,b) in zip(*gks): grad_ref[1,R:R+256,:]=jnp.where(lane<64,a,b).astype(bf16)
+    for (R,a),(_,b) in zip(*gvs): grad_ref[2,R:R+256,:]=jnp.where(lane<64,a,b).astype(bf16)
+    grad_ref[0]=(jnp.where(lane<64,dq_acc[0],dq_acc[1])*0.125).astype(bf16)
+
+def attn_bwd(packed,qa,o,do,g,bnd,half):
+    sp=lambda off: pl.BlockSpec((T,128),lambda i:(0,off+4*half+i))
     return pl.pallas_call(bwd_body,
-        grid=(8,),
+        grid=(4,),
         in_specs=[pl.BlockSpec(memory_space=pltpu.SMEM),
-                  pl.BlockSpec((1,2,256),lambda i:(i,0,0)),
-                  pl.BlockSpec((T,256),lambda i:(0,i)),sp(8),sp(16),sp(0),sp(0)],
-        out_specs=[sp(0),sp(0),sp(0),pl.BlockSpec((1,2,256),lambda i:(i,0,0))],
-        out_shape=[sh,sh,sh,jax.ShapeDtypeStruct((8,2,256),f32)],
+                  pl.BlockSpec((1,2,256),lambda i:(4*half+i,0,0)),
+                  pl.BlockSpec((T,256),lambda i:(0,4*half+i)),sp(8),sp(16),sp(0),sp(0)],
+        out_specs=[pl.BlockSpec((3,T,128),lambda i:(0,0,i)),pl.BlockSpec((1,2,256),lambda i:(i,0,0))],
+        out_shape=[jax.ShapeDtypeStruct((3,T,512),bf16),jax.ShapeDtypeStruct((4,2,256),f32)],
         scratch_shapes=[pltpu.VMEM((2,T,128),f32),pltpu.VMEM((128,256),f32)],
-        cost_estimate=pl.CostEstimate(flops=5*16*11*65536*128,bytes_accessed=24<<20,transcendentals=16*11*65536),
+        cost_estimate=pl.CostEstimate(flops=5*8*11*65536*128,bytes_accessed=12<<20,transcendentals=8*11*65536),
         compiler_params=pltpu.CompilerParams(vmem_limit_bytes=56<<20))(bnd,g,qa,packed,packed,o,do)
+
+
+def shape(*dims, dtype=bf16):
+    return jax.ShapeDtypeStruct(dims, dtype)
+
+
+def whole(*dims):
+    return pl.BlockSpec(dims, lambda i: (0,) * len(dims))
+
+
+def columns(rows, width, first=0):
+    return pl.BlockSpec((rows, width), lambda i: (0, first + i))
+
+
+SCALAR = pl.BlockSpec(memory_space=pltpu.SMEM)
+
+
+def call(body, grid, in_specs, out_specs, out_shape, scratch=(), flops=0, moved=0, aliases={}):
+    if not flops:
+        moved = 0
+    return pl.pallas_call(
+        body,
+        grid=(grid,),
+        in_specs=in_specs,
+        out_specs=out_specs,
+        out_shape=out_shape,
+        scratch_shapes=list(scratch),
+        input_output_aliases=aliases,
+        cost_estimate=pl.CostEstimate(flops=flops, bytes_accessed=moved, transcendentals=0),
+        compiler_params=pltpu.CompilerParams(vmem_limit_bytes=58 << 20),
+    )
+
+
+def row_stats(x):
+    mean = jnp.mean(x, axis=-1, keepdims=True)
+    center = x - mean
+    rstd = lax.rsqrt(jnp.mean(center * center, axis=-1, keepdims=True) + 1e-05)
+    return center * rstd, rstd
+
+
+def back_through_norm(xhat, rstd, scaled):
+    return rstd * (
+        scaled
+        - jnp.mean(scaled, axis=-1, keepdims=True)
+        - xhat * jnp.mean(scaled * xhat, axis=-1, keepdims=True)
+    )
+
+
+def shifted_rows(ext, offset, r):
+    fine = lax.rem(offset, 8)
+    rows = ext[pl.ds(pl.multiple_of(offset - fine + r, 8), 136), :]
+    return pltpu.roll(rows, lax.rem(136 - fine, 136), 0)[:128]
+
+
+def prep_body(start_ref, tok_ref, cot_ref, tok_out, cot_out, bias_out, ext):
+    start = start_ref[0]
+    for source, target in ((tok_ref, tok_out), (cot_ref, cot_out)):
+        for r in range(0, T, 256):
+            ext[r : r + 256, :] = source[r : r + 256, :].astype(f32)
+        ext[T : T + SHORT, :] = source[0:SHORT, :].astype(f32)
+        total = None
+        for r in range(0, T, 128):
+            rows = shifted_rows(ext, start, r)
+            target[r : r + 128, :] = rows.astype(bf16)
+            if target is cot_out:
+                part = jnp.sum(rows, axis=0, keepdims=True)
+                total = part if total is None else total + part
+    bias_out[...] = total
+
+
+def prep(start, tokens, cotangent):
+    return call(
+        prep_body, 1,
+        [SCALAR, whole(T, D), whole(T, D)],
+        [whole(T, D), whole(T, D), whole(1, D)],
+        [shape(T, D), shape(T, D), shape(1, D, dtype=f32)],
+        [pltpu.VMEM((T + SHORT + 8, D), f32)],
+        moved=11 << 20,
+    )(start, tokens, cotangent)
+
+
+def qkv_body(tok_ref, gain_ref, shift_ref, w_ref, packed_ref, normed_ref):
+    @pl.when(pl.program_id(0) == 0)
+    def _():
+        for r in range(0, T, 256):
+            xhat, _ = row_stats(tok_ref[r : r + 256, :].astype(f32))
+            normed_ref[r : r + 256, :] = (xhat * gain_ref[...] + shift_ref[...]).astype(bf16)
+
+    packed_ref[...] = dot(normed_ref[...], w_ref[...], NN).astype(bf16)
+
+
+def qkv_forward(tok, gain, shift, w_qkv):
+    return call(
+        qkv_body, 6,
+        [whole(T, D), whole(1, D), whole(1, D), columns(D, 512)],
+        [columns(T, 512), whole(T, D)],
+        [shape(T, 3 * D), shape(T, D)],
+        flops=6 * T * D * D, moved=20 << 20,
+    )(tok, gain, shift, w_qkv)
+
+
+PIECES = (
+    (0, 0, 128), (1, 0, 128), (2, 0, 128), (4, 0, 128), (6, 0, 64), (6, 64, 64),
+    (3, 0, 128), (5, 0, 128), (7, 0, 64), (7, 64, 64),
+)
+
+
+def qkv_pieces_body(me_ref, tok_ref, gain_ref, shift_ref, *refs):
+    pieces = refs[: len(PIECES)]
+    packed_ref, normed_ref, w_out, w_all, arrived, left = refs[len(PIECES) :]
+    step = pl.program_id(0)
+    save = pltpu.make_async_copy(w_all, w_out, left)
+
+    @pl.when(step == 0)
+    def _():
+        copies = []
+        for n, (other, first, rows) in enumerate(PIECES):
+            at = pl.multiple_of((me_ref[0] ^ other) * 128 + first, 64)
+            copy = pltpu.make_async_copy(pieces[n], w_all.at[pl.ds(at, rows), :], arrived.at[n])
+            copy.start()
+            copies.append(copy)
+        for r in range(0, T, 256):
+            xhat, _ = row_stats(tok_ref[r : r + 256, :].astype(f32))
+            normed_ref[r : r + 256, :] = (xhat * gain_ref[...] + shift_ref[...]).astype(bf16)
+        for copy in copies:
+            copy.wait()
+        save.start()
+
+    at = pl.multiple_of(step * 512, 512)
+    packed_ref[...] = dot(normed_ref[...], w_all[:, pl.ds(at, 512)], NN).astype(bf16)
+
+    @pl.when(step == pl.num_programs(0) - 1)
+    def _():
+        save.wait()
+
+
+def qkv_forward_pieces(me, tok, gain, shift, pieces):
+    anywhere = pl.BlockSpec(memory_space=pl.ANY)
+    return call(
+        qkv_pieces_body, 6,
+        [SCALAR, whole(T, D), whole(1, D), whole(1, D)] + [anywhere] * len(PIECES),
+        [columns(T, 512), whole(T, D), anywhere],
+        [shape(T, 3 * D), shape(T, D), shape(D, 3 * D)],
+        [
+            pltpu.VMEM((D, 3 * D), bf16),
+            pltpu.SemaphoreType.DMA((len(PIECES),)),
+            pltpu.SemaphoreType.DMA,
+        ],
+        flops=6 * T * D * D, moved=26 << 20,
+    )(me, tok, gain, shift, *pieces)
+
+
+def out_body(mixed_ref, w_ref, tok_ref, gain_ref, shift_ref, middle_ref, normed_ref):
+    middle = tok_ref[...].astype(f32) + dot(mixed_ref[...], w_ref[...], NN)
+    middle_ref[...] = middle
+    xhat, _ = row_stats(middle)
+    normed_ref[...] = (xhat * gain_ref[...] + shift_ref[...]).astype(bf16)
+
+
+def out_forward(mixed, w_out_up, tok, gain, shift):
+    rows = pl.BlockSpec((256, D), lambda i: (i, 0))
+    return call(
+        out_body, T // 256,
+        [rows, whole(D, D), rows, whole(1, D), whole(1, D)],
+        [rows, rows],
+        [shape(T, D, dtype=f32), shape(T, D)],
+        flops=2 * T * D * D, moved=16 << 20,
+    )(mixed, w_out_up, tok, gain, shift)
+
+
+C0 = float(np.sqrt(2.0 / np.pi))
+C1 = 0.044715 * C0
+
+
+def up_body(normed_ref, w_ref, bias_ref, activ_ref, slope_ref):
+    bias = bias_ref[...]
+    for r in range(0, T, 256):
+        u = dot(normed_ref[r : r + 256, :], w_ref[...], NN) + bias
+        square = u * u
+        half = 0.5 * jnp.tanh(u * (C0 + C1 * square)) + 0.5
+        activ = u * half
+        activ_ref[r : r + 256, :] = activ.astype(bf16)
+        slope = half + activ * (1.0 - half) * (2.0 * C0 + 6.0 * C1 * square)
+        slope_ref[r : r + 256, :] = slope.astype(bf16)
+
+
+def up_forward(normed_two, w_out_up, up_bias):
+    return call(
+        up_body, 8,
+        [whole(T, D), columns(D, 512, 2), columns(1, 512)],
+        [columns(T, 512), columns(T, 512)],
+        [shape(T, FF), shape(T, FF)],
+        flops=2 * T * D * FF, moved=32 << 20,
+    )(normed_two, w_out_up, up_bias)
+
+
+def grad_down_body(activ_ref, cot_ref, out_ref):
+    out_ref[0, 0] = dot(activ_ref[...], cot_ref[...], TN).astype(bf16).reshape(out_ref.shape[2:])
+
+
+def ffn_shape(ways):
+    return shape(ways, 2, 4, D // ways, D)
+
+
+def grad_down(activ, cot, ways):
+    rows = FF // ways
+    return call(
+        grad_down_body, ways,
+        [columns(T, rows), whole(T, D)],
+        pl.BlockSpec((1, 1, 4, D // ways, D), lambda i: (i, 0, 0, 0, 0)),
+        ffn_shape(ways),
+        flops=2 * T * D * FF, moved=21 << 20,
+    )(activ, cot)
+
+
+def grad_up_body(left_ref, right_ref, held_ref, out_ref):
+    value = dot(left_ref[...], right_ref[...], TN).astype(bf16)
+    out_ref[...] = value.reshape(out_ref.shape)
+
+
+def grad_up(left, right, held, ways):
+    return call(
+        grad_up_body, 8,
+        [whole(T, D), columns(T, 512), pl.BlockSpec(memory_space=pl.ANY)],
+        pl.BlockSpec((ways, 1, 1, D // ways, 512), lambda i: (0, 1, i // 2, 0, i % 2)),
+        ffn_shape(ways),
+        flops=2 * T * D * FF, moved=21 << 20, aliases={2: 0},
+    )(left, right, held)
+
+
+def grad_pre_body(cot_ref, w_ref, slope_ref, pre_ref, bias_ref):
+    total = None
+    for r in range(0, T, 256):
+        pre = (
+            dot(cot_ref[r : r + 256, :], w_ref[...], NT) * slope_ref[r : r + 256, :].astype(f32)
+        ).astype(bf16)
+        pre_ref[r : r + 256, :] = pre
+        part = jnp.sum(pre.astype(f32), axis=0, keepdims=True)
+        total = part if total is None else total + part
+    bias_ref[...] = total
+
+
+def grad_pre_of(cot, w_down, slope):
+    return call(
+        grad_pre_body, 8,
+        [whole(T, D), pl.BlockSpec((512, D), lambda i: (i, 0)), columns(T, 512)],
+        [columns(T, 512), columns(1, 512)],
+        [shape(T, FF), shape(1, FF, dtype=f32)],
+        flops=2 * T * D * FF, moved=32 << 20,
+    )(cot, w_down, slope)
+
+
+def grad_tile_body(left_ref, right_ref, out_ref):
+    right = right_ref[...]
+    right = right.reshape(right.shape[-2:])
+    out_ref[...] = dot(left_ref[...], right, TN).astype(bf16)
+
+
+def right_tiles(right):
+    if right.ndim == 3:
+        return right.shape[0], pl.BlockSpec((1, T, 512), lambda i: (i, 0, 0))
+    return right.shape[1] // 512, columns(T, 512)
+
+
+def grad_columns(left, right):
+    tiles, spec = right_tiles(right)
+    return call(
+        grad_tile_body, tiles,
+        [whole(T, D), spec],
+        columns(D, 512),
+        shape(D, tiles * 512),
+        flops=2 * T * D * tiles * 512, moved=T * (D + tiles * 512) * 2,
+    )(left, right)
+
+
+def take_blocks(me, left_ref, held, core):
+    for rel in range(4):
+        at = pl.multiple_of((((me >> 1) ^ rel) * 2 + core) * 128, 128)
+        held[:, 128 * rel : 128 * rel + 128] = left_ref[:, pl.ds(at, 128)]
+
+
+def tile_specs(lefts, rights):
+    specs, begins, first = [SCALAR], [], 0
+    for right in rights:
+        if right.ndim == 3:
+            count = right.shape[0]
+            spec = pl.BlockSpec(
+                (1, T, 512), lambda i, a=first, n=count: (jnp.clip(i - a, 0, n - 1), 0, 0)
+            )
+        else:
+            count = right.shape[1] // 512
+            spec = pl.BlockSpec(
+                (T, 512), lambda i, a=first, n=count: (0, jnp.clip(i - a, 0, n - 1))
+            )
+        specs.append(spec)
+        begins.append(first)
+        first += count
+    return specs + [whole(T, D)] * len(lefts), begins, first
+
+
+def block_products(me, core, begins, total, lefts, rights, held, emit):
+    step = pl.program_id(0)
+    for begin, end, left_ref, right_ref in zip(begins, begins[1:] + [total], lefts, rights):
+
+        @pl.when(step == begin)
+        def _():
+            take_blocks(me, left_ref, held, core)
+
+        @pl.when((step >= begin) & (step < end))
+        def _():
+            right = right_ref[...]
+            emit(dot(held[...], right.reshape(right.shape[-2:]), TN))
+
+
+def grad_theirs(me, lefts, rights):
+    specs, begins, tiles = tile_specs(lefts, rights)
+    n = len(lefts)
+
+    def body(me_ref, *refs):
+        out_ref, held = refs[2 * n :]
+
+        def emit(value):
+            out_ref[...] = value.astype(bf16)
+
+        me = me_ref[0]
+        block_products(me, 1 - (me & 1), begins, tiles, refs[n : 2 * n], refs[:n], held, emit)
+
+    return call(
+        body, tiles, specs, columns(512, 512), shape(512, tiles * 512),
+        [pltpu.VMEM((T, 512), bf16)],
+        flops=T * D * tiles * 512, moved=T * (D + tiles * 512) * 2,
+    )(me, *rights, *lefts)
+
+
+def grad_mine(me, lefts, rights, other):
+    specs, begins, tiles = tile_specs(lefts, rights)
+    n = len(lefts)
+
+    def body(me_ref, *refs):
+        other_ref, a_send, a_keep, b_send, b_keep, held = refs[2 * n :]
+
+        def emit(value):
+            total = (value + other_ref[...].astype(f32)).astype(bf16)
+            for rel, target, place in ((0, a_keep, 0), (1, a_send, 0), (2, a_keep, 1), (3, a_send, 1)):
+                target[place] = total[128 * rel : 128 * rel + 128, :256]
+            for rel, target, place in ((0, b_keep, 0), (1, b_keep, 1), (2, b_send, 0), (3, b_send, 1)):
+                target[place] = total[128 * rel : 128 * rel + 128, 256:]
+
+        me = me_ref[0]
+        block_products(me, me & 1, begins, tiles, refs[n : 2 * n], refs[:n], held, emit)
+
+    part = pl.BlockSpec((2, 128, 256), lambda i: (0, 0, i))
+    return call(
+        body, tiles, specs + [columns(512, 512)], [part] * 4, [shape(2, 128, tiles * 256)] * 4,
+        [pltpu.VMEM((T, 512), bf16)],
+        flops=T * D * tiles * 512, moved=T * (D + tiles * 512) * 2,
+    )(me, *rights, *lefts, other)
+
+
+def pair_sum_body(a_keep, a_got, b_keep, b_got, a_send, a_rest, b_send, b_rest):
+    for keep, got, send, rest in ((a_keep, a_got, a_send, a_rest), (b_keep, b_got, b_send, b_rest)):
+        for place, target in ((1, send), (0, rest)):
+            target[...] = (keep[place].astype(f32) + got[place].astype(f32)).astype(bf16)
+
+
+def pair_sum(*parts):
+    width = parts[0].shape[2]
+    return call(
+        pair_sum_body, 1,
+        [whole(2, 128, width)] * 4,
+        [whole(128, width)] * 4,
+        [shape(128, width)] * 4,
+        moved=128 * width * 24,
+    )(*parts)
+
+
+def add(a_ref, b_ref):
+    return a_ref[...].astype(f32) + b_ref[...].astype(f32)
+
+
+def last_sum_body(place_ref, a_keep, a_got, b_keep, b_got, send, keep):
+    bit = place_ref[0] & 1
+    for n, (one, two) in enumerate(((a_keep, a_got), (b_keep, b_got))):
+        for target, mine in ((keep, bit), (send, 1 - bit)):
+            at = pl.ds(pl.multiple_of(mine * 64, 64), 64)
+            total = (one[at, :].astype(f32) + two[at, :].astype(f32)).astype(bf16)
+            for tile in range(total.shape[1] // 256):
+                target[:, 512 * tile + 256 * n : 512 * tile + 256 * n + 256] = total[
+                    :, 256 * tile : 256 * tile + 256
+                ]
+
+
+def last_sum(place, *parts):
+    width = 2 * parts[0].shape[1]
+    return call(
+        last_sum_body, 1,
+        [SCALAR] + [whole(128, width // 2)] * 4,
+        [whole(64, width)] * 2,
+        [shape(64, width)] * 2,
+        moved=128 * width * 6,
+    )(place, *parts)
+
+
+def half_sum_body(place_ref, keep, got, send, rest):
+    bit = place_ref[0] >> 1
+    for target, mine in ((rest, bit), (send, 1 - bit)):
+        at = pl.ds(pl.multiple_of(mine * 32, 32), 32)
+        target[...] = (keep[at, :].astype(f32) + got[at, :].astype(f32)).astype(bf16)
+
+
+def half_sum(place, keep, got):
+    width = keep.shape[1]
+    return call(
+        half_sum_body, 1,
+        [SCALAR] + [whole(64, width)] * 2,
+        [whole(32, width)] * 2,
+        [shape(32, width)] * 2,
+        moved=64 * width * 6,
+    )(place, keep, got)
+
+
+def quarter_sum_body(keep, got, out):
+    out[...] = add(keep, got).astype(bf16)
+
+
+def quarter_sum(keep, got):
+    width = keep.shape[1]
+    return call(
+        quarter_sum_body, 1, [whole(32, width)] * 2, whole(32, width), shape(32, width),
+        moved=32 * width * 6,
+    )(keep, got)
+
+
+def widen_body(sum_ref, down_ref, up_ref):
+    rows = sum_ref.shape[3]
+    for k in range(4):
+        down_ref[rows * k : rows * k + rows, :] = sum_ref[0, 0, k].astype(f32)
+        up_ref[:, D * k : D * k + D] = sum_ref[0, 1, k].astype(f32)
+
+
+def widen(total):
+    rows = total.shape[3]
+    return call(
+        widen_body, 1,
+        [whole(*total.shape)],
+        [whole(4 * rows, D), whole(rows, FF)],
+        [shape(4 * rows, D, dtype=f32), shape(rows, FF, dtype=f32)],
+    )(total)
+
+
+def spread_body(place_ref, low_own, low_next, low_far, high_own, high_next, high_far, qkv_out, out_out):
+    one, two = place_ref[0] & 1, place_ref[0] >> 1
+    for own, near, far, half in ((low_own, low_next, low_far, 0), (high_own, high_next, high_far, 1)):
+        for ref, rows, bit_one, bit_two in (
+            (own, slice(0, 32), one, two),
+            (near, slice(0, 32), one, 1 - two),
+            (far, slice(0, 32), 1 - one, two),
+            (far, slice(32, 64), 1 - one, 1 - two),
+        ):
+            at = pl.ds(pl.multiple_of(bit_one * 64 + bit_two * 32, 32), 32)
+            for n in range(3):
+                first = 1024 * n + 512 * half
+                qkv_out[at, first : first + 512] = ref[rows, 512 * n : 512 * n + 512].astype(f32)
+            if half == 0:
+                out_out[at, :] = ref[rows, 1536:].astype(f32)
+
+
+def spread(place, *parts):
+    return call(
+        spread_body, 1,
+        [SCALAR] + [whole(*part.shape) for part in parts],
+        [whole(128, 3 * D), whole(128, D)],
+        [shape(128, 3 * D, dtype=f32), shape(128, D, dtype=f32)],
+        moved=128 * 4 * D * 6,
+    )(place, *parts)
+
+
+def mid_body(
+    pre_ref, up_ref, middle_ref, cot_ref, gain_ref, w_out_ref,
+    mid_ref, att_ref, mixed_ref, gain_out, shift_out, acc,
+):
+    step = pl.program_id(0)
+
+    @pl.when(step == 0)
+    def _():
+        acc[...] = dot(pre_ref[...], up_ref[...], NT)
+
+    @pl.when(step > 0)
+    def _():
+        acc[...] += dot(pre_ref[...], up_ref[...], NT)
+
+    @pl.when(step == pl.num_programs(0) - 1)
+    def _():
+        gains = shifts = None
+        for r in range(0, T, 256):
+            g = acc[r : r + 256, :]
+            xhat, rstd = row_stats(middle_ref[r : r + 256, :])
+            a = jnp.sum(g * xhat, axis=0, keepdims=True)
+            b = jnp.sum(g, axis=0, keepdims=True)
+            gains = a if gains is None else gains + a
+            shifts = b if shifts is None else shifts + b
+            mid = cot_ref[r : r + 256, :].astype(f32) + back_through_norm(
+                xhat, rstd, g * gain_ref[...]
+            )
+            mid_ref[r : r + 256, :] = mid
+            att = mid.astype(bf16)
+            att_ref[r : r + 256, :] = att
+            mixed_ref[r : r + 256, :] = dot(att, w_out_ref[...], NT).astype(bf16)
+        gain_out[...] = gains
+        shift_out[...] = shifts
+
+
+def grad_middle_of(grad_pre, w_out_up, middle, cot, gain):
+    return call(
+        mid_body, 8,
+        [
+            columns(T, 512), columns(D, 512, 2), whole(T, D), whole(T, D), whole(1, D),
+            whole(D, D),
+        ],
+        [whole(T, D), whole(T, D), whole(T, D), whole(1, D), whole(1, D)],
+        [
+            shape(T, D, dtype=f32), shape(T, D), shape(T, D),
+            shape(1, D, dtype=f32), shape(1, D, dtype=f32),
+        ],
+        [pltpu.VMEM((T, D), f32)],
+        flops=2 * T * D * FF + 2 * T * D * D, moved=42 << 20,
+    )(grad_pre, w_out_up, middle, cot, gain, w_out_up)
+
+
+def unrotate(ext, start, out_ref):
+    ext[0:SHORT, :] = ext[T : T + SHORT, :]
+    for r in range(0, T, 128):
+        out_ref[r : r + 128, :] = shifted_rows(ext, SHORT - start, r).astype(bf16)
+
+
+def tok_body(
+    start_ref, low_ref, high_ref, w_ref, tok_ref, mid_ref, gain_ref, grad_ref, gain_out, shift_out, ext
+):
+    step = pl.program_id(0)
+
+    @pl.when(step == 0)
+    def _():
+        ext[SHORT : SHORT + T, :] = dot(low_ref[0], w_ref[...], NT)
+
+    @pl.when((step > 0) & (lax.rem(step, 2) == 0))
+    def _():
+        ext[SHORT : SHORT + T, :] += dot(low_ref[0], w_ref[...], NT)
+
+    @pl.when(lax.rem(step, 2) == 1)
+    def _():
+        ext[SHORT : SHORT + T, :] += dot(high_ref[0], w_ref[...], NT)
+
+    @pl.when(step == pl.num_programs(0) - 1)
+    def _():
+        gains = shifts = None
+        for r in range(0, T, 256):
+            g = ext[SHORT + r : SHORT + r + 256, :]
+            xhat, rstd = row_stats(tok_ref[r : r + 256, :].astype(f32))
+            a = jnp.sum(g * xhat, axis=0, keepdims=True)
+            b = jnp.sum(g, axis=0, keepdims=True)
+            gains = a if gains is None else gains + a
+            shifts = b if shifts is None else shifts + b
+            ext[SHORT + r : SHORT + r + 256, :] = mid_ref[r : r + 256, :] + back_through_norm(
+                xhat, rstd, g * gain_ref[...]
+            )
+        unrotate(ext, start_ref[0], grad_ref)
+        gain_out[...] = gains
+        shift_out[...] = shifts
+
+
+def grad_tokens_of(start, low, high, w_qkv, tok, mid, gain):
+    half = pl.BlockSpec((1, T, 512), lambda i: (i // 2, 0, 0))
+    return call(
+        tok_body, 6,
+        [
+            SCALAR, half, half, columns(D, 512), whole(T, D), whole(T, D), whole(1, D),
+        ],
+        [whole(T, D), whole(1, D), whole(1, D)],
+        [shape(T, D), shape(1, D, dtype=f32), shape(1, D, dtype=f32)],
+        [pltpu.VMEM((T + SHORT + 8, D), f32)],
+    )(start, low, high, w_qkv, tok, mid, gain)
+
+
+def output_body(start_ref, activ_ref, w_ref, middle_ref, bias_ref, out_ref, ext):
+    step = pl.program_id(0)
+
+    @pl.when(step == 0)
+    def _():
+        ext[SHORT : SHORT + T, :] = middle_ref[...] + bias_ref[...]
+
+    ext[SHORT : SHORT + T, :] += dot(activ_ref[...], w_ref[...], NN)
+
+    @pl.when(step == pl.num_programs(0) - 1)
+    def _():
+        unrotate(ext, start_ref[0], out_ref)
+
+
+def output_of(start, activ, w_down, middle, bias):
+    return call(
+        output_body, 4,
+        [
+            SCALAR, columns(T, 1024), pl.BlockSpec((1024, D), lambda i: (i, 0)), whole(T, D),
+            whole(1, D),
+        ],
+        whole(T, D),
+        shape(T, D),
+        [pltpu.VMEM((T + SHORT + 8, D), f32)],
+    )(start, activ, w_down, middle, bias)
 
 
 def bucket_edges(bucket_count, reach_max):
@@ -203,23 +826,35 @@
     return hot.astype(np.float32)
 
 
-def gelu_tanh(values):
-    return jax.nn.gelu(values, approximate=True)
-
-
-def norm_stats(values):
-    mean = jnp.mean(values, axis=-1, keepdims=True)
-    center = values - mean
-    spread = jnp.mean(center * center, axis=-1, keepdims=True)
-    return center * lax.rsqrt(spread + 1e-05), lax.rsqrt(spread + 1e-05)
-
-
-def norm_back(xhat, rstd, scaled):
-    return rstd * (
-        scaled
-        - jnp.mean(scaled, axis=-1, keepdims=True)
-        - xhat * jnp.mean(scaled * xhat, axis=-1, keepdims=True)
-    )
+def swap(a, bit):
+    return lax.ppermute(a, "fsdp", [(i, i ^ bit) for i in range(8)])
+
+
+def swap_rep(a, bit):
+    return lax.ppermute(a, "rep", [(i, i ^ bit) for i in range(4)])
+
+
+def gather_small(small):
+    n = lax.axis_size("fsdp")
+    if n != 8:
+        return lax.all_gather(small, "fsdp", axis=0)
+    me = lax.axis_index("fsdp")
+    held = small[None]
+    for bit in (1, 2, 4):
+        other = swap(held, bit)
+        upper = (me & bit) != 0
+        held = jnp.concatenate(
+            [jnp.where(upper, other, held), jnp.where(upper, held, other)], axis=0
+        )
+    return held
+
+
+def after(value, *others):
+    return lax.optimization_barrier((value,) + others)[0]
+
+
+def after_all(values, *others):
+    return lax.optimization_barrier(tuple(values) + others)[: len(values)]
 
 
 def local(
@@ -228,92 +863,121 @@
 ):
     gather = lambda a: lax.all_gather(a, "fsdp", axis=0, tiled=True)
     pieces = (attn_gain, attn_shift, ffn_gain, ffn_shift, down_bias, up_bias, rel_table.reshape(-1))
-    small = jnp.concatenate(pieces).reshape(1, -1)
-    small_full = gather(small)
-    qkv_full = gather(w_qkv)
-    out_full = gather(w_out)
-    up_full = gather(w_up)
-    down_full = gather(w_down)
     cuts = np.cumsum([0] + [piece.size for piece in pieces])
+    rows = -(-int(cuts[-1]) // 2048) * 16
+    small = jnp.concatenate(pieces + (jnp.zeros((rows * 128 - int(cuts[-1]),), bf16),))
+    small_full = gather_small(small.reshape(rows, 128))
     ways = small_full.shape[0]
-    part = lambda i: small_full[:, cuts[i] : cuts[i + 1]].reshape(-1).astype(jnp.float32)
+    small_full = small_full.reshape(ways, rows * 128)
+    me = lax.axis_index("fsdp").astype(jnp.int32).reshape(1)
+    by_pieces = ways == 8 and lax.axis_size("rep") == 4
+    lens = item_lengths[0]
+    first, second = lens[0], lens[1]
+    long_first = first == LONG
+    long_mid = second == LONG
+    start = jnp.where(long_first, 0, jnp.where(long_mid, first, first + second)).reshape(1)
+    bound = jnp.where(long_first, second, jnp.where(long_mid, lens[2], first)).reshape(1)
+    tok, cot, grad_down_bias = prep(start, tokens, cotangent)
+    out_up_own = jnp.concatenate([w_out, w_up], axis=1)
+    if by_pieces:
+        from_core, from_x, from_y = swap(w_qkv, 1), swap(w_qkv, 2), swap(w_qkv, 4)
+        from_x, from_y = after_all((from_x, from_y), tok, out_up_own)
+        top, bottom = swap(from_x[:64], 4), swap(from_y[64:], 2)
+        out_up_own = after(out_up_own, top, bottom)
+        qkv_pieces = (
+            w_qkv, from_core, from_x, from_y, top, bottom,
+            swap(from_x, 1), swap(from_y, 1), swap(top, 1), swap(bottom, 1),
+        )
+    out_up = gather(out_up_own)
+    part = lambda i: small_full[:, cuts[i] : cuts[i + 1]].reshape(1, -1).astype(f32)
     gain_one, shift_one, gain_two, shift_two, down_bias_full, up_bias_full = (
         part(i) for i in range(6)
     )
     table = part(6).reshape(NBUCKET, H)
-    lens = item_lengths[0]
-    first, second = lens[0], lens[1]
-    long_first = first == LONG
-    long_mid = second == LONG
-    start = jnp.where(long_first, 0, jnp.where(long_mid, first, first + second))
-    bound = jnp.where(long_first, second, jnp.where(long_mid, lens[2], first)).reshape(1)
-    rotate = lambda a, by: jnp.roll(a, by, axis=0)
-    tok = rotate(tokens, -start)
-    cot = rotate(cotangent, -start)
     relative = table - table[NBUCKET - 1 :]
     reach = np.arange(256)
     fwd_hot = onehot_bucket(np.maximum(128 - reach, 0), reach <= 128)
     bwd_hot = onehot_bucket(reach, reach < 129)
     spread_of = lambda hot: jnp.dot(
-        relative.T, hot, precision=lax.Precision.HIGHEST, preferred_element_type=jnp.float32
+        relative.T, hot, precision=lax.Precision.HIGHEST, preferred_element_type=f32
     ).reshape(8, 2, 256)
     bias_fwd, bias_bwd = spread_of(fwd_hot), spread_of(bwd_hot)
 
-    hidden = tok.astype(jnp.float32)
-    xhat_one, rstd_one = norm_stats(hidden)
-    normed = (xhat_one * gain_one + shift_one).astype(jnp.bfloat16)
-    packed = jnp.dot(normed, qkv_full, preferred_element_type=jnp.float32).astype(jnp.bfloat16)
+    scatter = lambda a: lax.psum_scatter(a, "fsdp", scatter_dimension=0, tiled=True)
+    total = lambda a: lax.psum(a, "rep")
+
+    if by_pieces:
+        qkv_pieces = after_all(qkv_pieces, bias_fwd, gain_two)
+        packed, normed, qkv_full = qkv_forward_pieces(me, tok, gain_one, shift_one, qkv_pieces)
+    else:
+        qkv_full = gather(w_qkv)
+        packed, normed = qkv_forward(tok, gain_one, shift_one, qkv_full)
+
+    def begin(lefts, rights):
+        return swap(grad_theirs(me, lefts, rights), 1)
+
+    def second(lefts, rights, other):
+        a_send, a_keep, b_send, b_keep = grad_mine(me, lefts, rights, other)
+        return a_keep, swap(a_send, 2), b_keep, swap(b_send, 4)
+
+    def third(parts):
+        a_send, a_keep, b_send, b_keep = pair_sum(*parts)
+        return a_keep, swap(a_send, 4), b_keep, swap(b_send, 2)
+
+    place = lax.axis_index("rep").astype(jnp.int32).reshape(1)
+
+    def along_one(parts):
+        send, keep = last_sum(place, *parts)
+        return keep, swap_rep(send, 1)
+
+    def along_two(parts):
+        send, keep = half_sum(place, *parts)
+        return keep, swap_rep(send, 2)
+
     mixed, query_aug = attn_fwd(packed, bias_fwd, bound)
-    middle = hidden + jnp.dot(mixed, out_full, preferred_element_type=jnp.float32)
-    xhat_two, rstd_two = norm_stats(middle)
-    normed_two = (xhat_two * gain_two + shift_two).astype(jnp.bfloat16)
-    pre_act = (
-        jnp.dot(normed_two, up_full, preferred_element_type=jnp.float32) + up_bias_full
+    down_full = gather(after(w_down, mixed, out_up))
+    middle, normed_two = out_forward(mixed, out_up, tok, gain_two, shift_two)
+    activ, slope = up_forward(normed_two, out_up, up_bias_full)
+    grad_w_ffn = grad_down(activ, cot, ways)
+    grad_pre, grad_up_bias = grad_pre_of(after(cot, grad_w_ffn), down_full, slope)
+    grad_w_ffn = grad_up(normed_two, grad_pre, grad_w_ffn, ways)
+    share_ffn = scatter(grad_w_ffn)
+    grad_middle, grad_att, grad_mixed, grad_ffn_gain, grad_ffn_shift = grad_middle_of(
+        after(grad_pre, grad_w_ffn), out_up, middle, cot, gain_two
     )
-    activ = gelu_tanh(pre_act).astype(jnp.bfloat16)
-    cot_float = cot.astype(jnp.float32)
-    grad_w_down = jnp.einsum("tf,td->fd", activ, cot, preferred_element_type=jnp.float32)
-    grad_down_bias = jnp.sum(cot_float, axis=0)
-    scatter = lambda a: lax.psum_scatter(
-        a.astype(jnp.bfloat16), "fsdp", scatter_dimension=0, tiled=True
+    low, reach_low = attn_bwd(packed, query_aug, mixed, grad_mixed, bias_bwd, bound, 0)
+    if by_pieces:
+        pair = (normed, mixed), (low, grad_att)
+        low_other = begin(*pair)
+        packed_next = after(packed, low_other)
+    else:
+        packed_next = after(packed, low)
+    high, reach_high = attn_bwd(
+        packed_next, query_aug, mixed, grad_mixed, bias_bwd, bound, 1
     )
-    share_down = scatter(grad_w_down)
-    grad_activ = jnp.einsum("td,fd->tf", cot, down_full, preferred_element_type=jnp.float32)
-    grad_pre = jax.vjp(gelu_tanh, pre_act)[1](grad_activ)[0].astype(jnp.bfloat16)
-    grad_w_up = jnp.einsum("td,tf->df", normed_two, grad_pre, preferred_element_type=jnp.float32)
-    share_up = scatter(grad_w_up)
-    grad_up_bias = jnp.sum(grad_pre.astype(jnp.float32), axis=0)
-    grad_normed_two = jnp.einsum("tf,df->td", grad_pre, up_full, preferred_element_type=jnp.float32)
-    grad_ffn_gain = jnp.sum(grad_normed_two * xhat_two, axis=0)
-    grad_ffn_shift = jnp.sum(grad_normed_two, axis=0)
-    grad_middle = cot_float + norm_back(xhat_two, rstd_two, grad_normed_two * gain_two)
-    grad_attended = grad_middle.astype(jnp.bfloat16)
-    grad_w_out = jnp.einsum("td,te->de", mixed, grad_attended, preferred_element_type=jnp.float32)
-    share_out = scatter(grad_w_out)
-    grad_mixed = jnp.einsum(
-        "te,de->td", grad_attended, out_full, preferred_element_type=jnp.float32
-    ).astype(jnp.bfloat16)
-    gq, gk, gv, grad_reach = attn_bwd(packed, query_aug, mixed, grad_mixed, bias_bwd, bound)
-    grad_packed = jnp.concatenate([gq, gk, gv], axis=1)
+    grad_reach = jnp.concatenate([reach_low, reach_high], axis=0)
     near_hot = onehot_bucket(reach, reach < EDGES[-1])
     grad_near = jnp.dot(
         near_hot, grad_reach.reshape(H, 256).T,
-        precision=lax.Precision.HIGHEST, preferred_element_type=jnp.float32,
+        precision=lax.Precision.HIGHEST, preferred_element_type=f32,
     )
     far = (np.arange(NBUCKET) == NBUCKET - 1).astype(np.float32)[:, None]
     grad_rel_table = grad_near - far * jnp.sum(grad_near, axis=0, keepdims=True)
-    grad_w_qkv = jnp.einsum("td,te->de", normed, grad_packed, preferred_element_type=jnp.float32)
-    share_qkv = scatter(grad_w_qkv)
-    grad_normed = jnp.einsum("te,de->td", grad_packed, qkv_full, preferred_element_type=jnp.float32)
-    grad_attn_gain = jnp.sum(grad_normed * xhat_one, axis=0)
-    grad_attn_shift = jnp.sum(grad_normed, axis=0)
-    grad_tokens = (
-        grad_middle + norm_back(xhat_one, rstd_one, grad_normed * gain_one)
-    ).astype(jnp.bfloat16)
-    grad_tokens = rotate(grad_tokens, start)
-    ffn_out = jnp.dot(activ, down_full, preferred_element_type=jnp.float32) + down_bias_full
-    output = rotate((middle + ffn_out).astype(jnp.bfloat16), start)
-
+    if by_pieces:
+        high_other = begin((normed,), (high,))
+        low_parts = second(pair[0], (low, after(grad_att, high_other)), low_other)
+        high_parts = second((normed,), (after(high, low_parts[0]),), high_other)
+        low_sent = low_parts[0]
+        low_parts = third(low_parts)
+        high_next = after(high, high_parts[0], low_parts[0])
+    else:
+        share_low = scatter(grad_columns(normed, low))
+        share_high = scatter(grad_columns(normed, high))
+        share_out = scatter(grad_columns(mixed, grad_att))
+        low_sent = high_next = high
+    grad_tokens, grad_attn_gain, grad_attn_shift = grad_tokens_of(
+        start, low, high_next, qkv_full, tok, grad_middle, gain_one
+    )
     flat = lambda a: a.reshape(ways, -1)
     vectors = jnp.concatenate(
         [
@@ -322,15 +986,42 @@
         ],
         axis=1,
     )
-    share_small = lax.psum_scatter(
-        vectors.astype(jnp.bfloat16), "fsdp", scatter_dimension=0, tiled=True
-    )
-    total = lambda a: lax.psum(a, "rep").astype(jnp.float32)
-    sum_small = total(share_small)
-    cut = lambda i: sum_small[0, cuts[i] : cuts[i + 1]]
+    activ_next = after(activ, grad_tokens)
+    if by_pieces:
+        high_parts = third(after_all(high_parts, grad_tokens))
+        low_parts = along_one(after_all(low_parts, grad_tokens))
+        activ_next = after(activ_next, low_parts[0], high_parts[0])
+    sum_down, sum_up = widen(total(after(share_ffn, low_sent)))
+    output = output_of(start, activ_next, down_full, middle, down_bias_full)
+    if by_pieces:
+        for bit in (1, 2, 4):
+            vectors = vectors + swap(vectors, bit)
+        mine = lax.dynamic_slice_in_dim(vectors, lax.axis_index("fsdp"), 1, 0)
+        for bit in (1, 2):
+            mine = mine + swap_rep(mine, bit)
+        low_parts = along_two(after_all(low_parts, output))
+        high_parts = along_one(after_all(high_parts, output))
+        low_own = quarter_sum(*low_parts)
+        high_parts = along_two(after_all(high_parts, sum_down, sum_up))
+        low_next = swap_rep(low_own, 2)
+        high_own = quarter_sum(*high_parts)
+        high_next = swap_rep(high_own, 2)
+        low_far = swap_rep(jnp.concatenate([low_own, low_next], axis=0), 1)
+        high_far = swap_rep(jnp.concatenate([high_own, high_next], axis=0), 1)
+        sum_qkv, sum_out = spread(
+            place, low_own, low_next, low_far, high_own, high_next, high_far
+        )
+    else:
+        mine = total(scatter(vectors))
+        sum_out = total(share_out)
+        sum_qkv = jnp.stack(
+            [total(share_low).reshape(-1, 3, 512), total(share_high).reshape(-1, 3, 512)], axis=2
+        ).reshape(-1, 3 * D)
+    cut = lambda i: mine[0, cuts[i] : cuts[i + 1]]
     return (
-        output, grad_tokens, cut(0), cut(1), total(share_qkv), cut(6).reshape(-1, H),
-        total(share_out), cut(2), cut(3), total(share_up), cut(5), total(share_down), cut(4),
+        output, grad_tokens, cut(0), cut(1), sum_qkv.astype(f32), cut(6).reshape(-1, H),
+        sum_out.astype(f32), cut(2), cut(3), sum_up, cut(5),
+        sum_down, cut(4),
     )
 
 

time: 690 us -> 476 us (0.69)
  Pallas kernels: 75.3 us -> 321 us
  waiting for transfers between devices: 266 us -> 71.6 us
  matrix products: 192 us -> 0.5 us
  blocking collectives: 62 us -> 0 us
  starting transfers between devices: 0.36 us -> 36.8 us
  other arithmetic: 38.5 us -> 2.51 us
  local copies, waits for them, and re-layouts: 25.3 us -> 15.2 us
    pallas_call x1 -> x26, Pallas kernels: 41.7 us -> 288 us  [the longest x2 45.2 us: attn_bwd(): pl.pallas_call(bwd_body, grid=(4,), in_specs=[pl.BlockSpec(memory_space=p...]
    dot_general x12 -> x0, matrix products: 190 us -> none  [the longest x1 30.1 us: local(): jnp.einsum('td,fd->tf', cot, down_full, preferred_element_type=jnp.float32)]
    reduce_scatter x4 -> x1, waiting for transfers between devices: 108 us -> 2.58 us  [local(): lax.psum_scatter(a, 'fsdp', scatter_dimension=0, tiled=True)]
    psum x1, waiting for transfers between devices: 95.6 us -> 0.01 us  [local(): total = lambda a: lax.psum(a, 'rep')]
    ppermute x0 -> x35, waiting for transfers between devices: none -> 66.2 us  [the longest x25 41.7 us: swap(): return lax.ppermute(a, 'fsdp', [(i, i ^ bit) for i in range(8)])]
    all_gather x4 -> x2, waiting for transfers between devices: 60.2 us -> 2.74 us  [local(): gather = lambda a: lax.all_gather(a, 'fsdp', axis=0, tiled=True)]
    unnamed x2 -> x0, blocking collectives: 50.1 us -> none
    ppermute x0 -> x35, starting transfers between devices: none -> 35.7 us  [the longest x25 20.3 us: swap(): return lax.ppermute(a, 'fsdp', [(i, i ^ bit) for i in range(8)])]
  transfers between devices with their start and end apart: 9 -> 39, of which waited for: 5 -> 27; matrix products, arithmetic and copies ran while one was open for 26% -> 2% of each run, Pallas kernels for 11% -> 61%
where the time goes in v2:
time: 476 us; the launch traced here: 468 us
  Pallas kernels  321 us (67%)
  waiting for transfers between devices  71.6 us (15%)
  starting transfers between devices  36.8 us (8%)
  between operations  19.9 us (4%)
  local copies, waits for them, and re-layouts  15.2 us (3%)
    pallas_call x2, Pallas kernels, attn_bwd(): pl.pallas_call(bwd_body, grid=(4,), in_specs=[pl.BlockSpec(memory_space=p...  45.2 us
    ppermute x25, waiting for transfers between devices, swap(): return lax.ppermute(a, 'fsdp', [(i, i ^ bit) for i in range(8)])  41.7 us
    pallas_call x1, Pallas kernels, attn_fwd(): pl.pallas_call(fwd_body, grid=(8,), in_specs=[pl.BlockSpec(memory_space=p...  33.8 us
    pallas_call x1, Pallas kernels, grad_middle_of(): call(mid_body, 8, [columns(T, 512), columns(D, 512, 2), whole(T, D), whol...  29.4 us
    pallas_call x1, Pallas kernels, up_forward(): call(up_body, 8, [whole(T, D), columns(D, 512, 2), columns(1, 512)], [col...  25 us
    ppermute x10, waiting for transfers between devices, swap_rep(): return lax.ppermute(a, 'rep', [(i, i ^ bit) for i in range(4)])  24.4 us
    pallas_call x1, Pallas kernels, grad_tokens_of(): call(tok_body, 6, [SCALAR, half, half, columns(D, 512), whole(T, D), whol...  22.8 us
    ppermute x25, starting transfers between devices, swap(): return lax.ppermute(a, 'fsdp', [(i, i ^ bit) for i in range(8)])  20.3 us
  transfers between devices with their start and end apart: 39, of which 27 were waited for; matrix products, arithmetic and copies ran while one was open for 2% of the time, Pallas kernels for 61%

profile of v2, /device:TPU:0, one launch (start us, length us, event | category | flops | bytes accessed | tf_op | source)
XLA Modules:
  0.0 467.9 jit_solution(10466696369727715083)
XLA Ops:
  7.2 3.0 collective-permute-start.4
  16.4 10.1 %shard_map.273 = (bf16[1280,1024]{1,0:T(8,128)(2,1)}, bf16[1280,1024]{1,0:T(8,128)(2,1)}, f32[1,1024]{1,0:T(1,128)}) custom-call(s32[1]{0:T(128)} %bitcast.2.start_ref, bf16[1280,1024]{1,0:T(8,128)(2,1)} %tok_ref.1, bf16[1280,1024]{1,0:T(8,128)(2,1)} %cot_ref.1), custom_call_target="tpu_custom_call" | custom-call | tf_op jit(solution)/shard_map/pallas_call | solution.py:267
  31.7 7.5 %collective-permute-done.6.refs_4_ = bf16[64,3072]{1,0:T(8,128)(2,1)S(1)} collective-permute-done((bf16[64,3072]{1,0:T(8,128)(2,1)S(1)}, bf16[64,3072]{1,0:T(8,128)(2,1)S(1)}, u32[]{:S(2)}, u32[]{:S(2)}) %collective-permute-start.6) | collective-permute-done | bytes 393248 | tf_op jit(solution)/shard_map/ppermute | solution.py:830
  43.0 3.0 collective-permute-done.1
  52.0 2.0 collective-permute-done.10.refs_8_
  55.2 16.0 %shard_map.274 = (bf16[1280,3072]{1,0:T(8,128)(2,1)}, bf16[1280,1024]{1,0:T(8,128)(2,1)}, bf16[1024,3072]{1,0:T(8,128)(2,1)}) custom-call(s32[1]{0:T(128)} %bitcast.10.me_ref, bf16[1280,1024]{1,0:T(8,128)(2,1)} %get-tuple-element.106.tok_ref, f32[1,1024]{1,0:T(1,128)} %bitcast.67, f32[1,1024]{1,0:T(1,128)} %bitcast.69, bf16[128,3072]{1,0:T(8,128)(2,1)} %refs_0_, ...), custom_call_target="tpu_custom_call" | custom-call | flops 8053063680 | bytes 27262976 | tf_op jit(solution)/shard_map/pallas_call | solution.py:334
  71.1 33.8 %shard_map.275 = (bf16[1280,1024]{1,0:T(8,128)(2,1)S(1)}, bf16[1280,2048]{1,0:T(8,128)(2,1)}) custom-call(s32[1]{0:T(128)} %bitcast.4.bnd_ref, f32[8,2,256]{2,1,0:T(2,128)S(1)} %copy.37.g_ref, bf16[1280,3072]{1,0:T(8,128)(2,1)} %get-tuple-element.136.q_ref.k_ref.v_ref, bf16[1280,3072]{1,0:T(8,128)(2,1)} %get-tuple-element.136.q_ref.k_ref.v_ref, ...), custom_call_target="tpu_custom_call" | custom-call | flops 2952790016 | bytes 16777216 | tf_op jit(solution)/shard_map/pallas_call | solution.py:96
  107.5 9.0 %shard_map.276 = (f32[1280,1024]{1,0:T(8,128)}, bf16[1280,1024]{1,0:T(8,128)(2,1)}) custom-call(bf16[1280,1024]{1,0:T(8,128)(2,1)} %copy-done, bf16[1024,5120]{1,0:T(8,128)(2,1)} %all-gather.3.cloned.1.call-done.w_ref.up_ref.w_out_ref, bf16[1280,1024]{1,0:T(8,128)(2,1)} %get-tuple-element.106.tok_ref, f32[1,1024]{1,0:T(1,128)} %bitcast.62, f32[1,1024]{1,0:T(1,128)} %bitcast.64), custom_call_target="tpu_custom_call" | custom-call | flops 2684354560 | bytes 16777216 | tf_op jit(solution)/shard_map/pallas_call | solution.py:357
  116.5 25.0 %shard_map.277 = (bf16[1280,4096]{1,0:T(8,128)(2,1)}, bf16[1280,4096]{1,0:T(8,128)(2,1)}) custom-call(bf16[1280,1024]{1,0:T(8,128)(2,1)} %get-tuple-element.122.normed_ref.left_ref, bf16[1024,5120]{1,0:T(8,128)(2,1)} %all-gather.3.cloned.1.call-done.w_ref.up_ref.w_out_ref, f32[1,4096]{1,0:T(1,128)} %bitcast.65), custom_call_target="tpu_custom_call" | custom-call | flops 10737418240 | bytes 33554432 | tf_op jit(solution)/shard_map/pallas_call | solution.py:383
  141.5 16.3 %shard_map.278.held_ref = bf16[8,2,4,128,1024]{4,3,2,1,0:T(8,128)(2,1)} custom-call(bf16[1280,4096]{1,0:T(8,128)(2,1)} %get-tuple-element.167.activ_ref, bf16[1280,1024]{1,0:T(8,128)(2,1)} %get-tuple-element.126.cot_ref), custom_call_target="tpu_custom_call" | custom-call | flops 10737418240 | bytes 22020096 | tf_op jit(solution)/shard_map/pallas_call | solution.py:402
  157.8 2.7 all-gather.5.cloned.1.call-done.w_ref
  160.5 19.0 %shard_map.279 = (bf16[1280,4096]{1,0:T(8,128)(2,1)}, f32[1,4096]{1,0:T(1,128)}) custom-call(bf16[1280,1024]{1,0:T(8,128)(2,1)} %get-tuple-element.126.cot_ref, bf16[4096,1024]{1,0:T(8,128)(2,1)} %all-gather.5.cloned.1.call-done.w_ref, bf16[1280,4096]{1,0:T(8,128)(2,1)} %get-tuple-element.128.slope_ref), custom_call_target="tpu_custom_call" | custom-call | flops 10737418240 | bytes 33554432 | tf_op jit(solution)/shard_map/pallas_call | solution.py:439
  179.5 16.2 %shard_map.280 = bf16[8,2,4,128,1024]{4,3,2,1,0:T(8,128)(2,1)} custom-call(bf16[1280,1024]{1,0:T(8,128)(2,1)} %get-tuple-element.122.normed_ref.left_ref, bf16[1280,4096]{1,0:T(8,128)(2,1)} %get-tuple-element.130.right_ref.pre_ref, bf16[8,2,4,128,1024]{4,3,2,1,0:T(8,128)(2,1)} %shard_map.278.held_ref), custom_call_target="tpu_custom_call", output_to_operand_aliasing={{}: (2, {})} | custom-call | flops 10737418240 | bytes 22020096 | tf_op jit(solution)/shard_map/pallas_call | solution.py:417
  197.2 29.4 %shard_map.281 = (f32[1280,1024]{1,0:T(8,128)}, bf16[1280,1024]{1,0:T(8,128)(2,1)}, bf16[1280,1024]{1,0:T(8,128)(2,1)}, f32[1,1024]{1,0:T(1,128)}, f32[1,1024]{1,0:T(1,128)}) custom-call(bf16[1280,4096]{1,0:T(8,128)(2,1)} %get-tuple-element.130.right_ref.pre_ref, bf16[1024,5120]{1,0:T(8,128)(2,1)} %all-gather.3.cloned.1.call-done.w_ref.up_ref.w_out_ref, ...), custom_call_target="tpu_custom_call" | custom-call | flops 13421772800 | bytes 44040192 | tf_op jit(solution)/shard_map/pallas_call | solution.py:709
  226.7 22.1 %shard_map.282 = (bf16[3,1280,512]{2,1,0:T(8,128)(2,1)}, f32[4,2,256]{2,1,0:T(2,128)}) custom-call(s32[1]{0:T(128)} %bitcast.4.bnd_ref, f32[8,2,256]{2,1,0:T(2,128)} %copy.39.g_ref, bf16[1280,2048]{1,0:T(8,128)(2,1)} %get-tuple-element.124.qa_ref, bf16[1280,3072]{1,0:T(8,128)(2,1)} %get-tuple-element.136.q_ref.k_ref.v_ref, ...), custom_call_target="tpu_custom_call" | custom-call | flops 3690987520 | bytes 12582912 | tf_op jit(solution)/shard_map/pallas_call | solution.py:186
  248.8 10.4 %shard_map.283 = bf16[512,2560]{1,0:T(8,128)(2,1)} custom-call(s32[1]{0:T(128)} %bitcast.10.me_ref, bf16[3,1280,512]{2,1,0:T(8,128)(2,1)} %get-tuple-element.133.refs_0_.low_ref, bf16[1280,1024]{1,0:T(8,128)(2,1)} %get-tuple-element.138.refs_1_, bf16[1280,1024]{1,0:T(8,128)(2,1)} %get-tuple-element.135.refs_2_.refs_1_, bf16[1280,1024]{1,0:T(8,128)(2,1)} %copy-done), custom_call_target="tpu_custom_call" | custom-call | flops 3355443200 | bytes 9175040 | tf_op jit(solution)/shard_map/pallas_call | solution.py:523
  259.4 5.0 %collective-permute-done.12.refs_4_ = bf16[512,2560]{1,0:T(8,128)(2,1)S(1)} collective-permute-done((bf16[512,2560]{1,0:T(8,128)(2,1)}, bf16[512,2560]{1,0:T(8,128)(2,1)S(1)}, u32[]{:S(2)}, u32[]{:S(2)}) %collective-permute-start.12) | collective-permute-done | bytes 2621472 | tf_op jit(solution)/shard_map/ppermute | solution.py:830
  264.3 23.1 %shard_map.284 = (bf16[3,1280,512]{2,1,0:T(8,128)(2,1)}, f32[4,2,256]{2,1,0:T(2,128)}) custom-call(s32[1]{0:T(128)} %bitcast.4.bnd_ref, f32[8,2,256]{2,1,0:T(2,128)} %copy.39.g_ref, bf16[1280,2048]{1,0:T(8,128)(2,1)} %get-tuple-element.124.qa_ref, bf16[1280,3072]{1,0:T(8,128)(2,1)} %get-tuple-element.136.q_ref.k_ref.v_ref, ...), custom_call_target="tpu_custom_call" | custom-call | flops 3690987520 | bytes 12582912 | tf_op jit(solution)/shard_map/pallas_call | solution.py:186
  287.4 6.8 %shard_map.285 = bf16[512,1536]{1,0:T(8,128)(2,1)} custom-call(s32[1]{0:T(128)} %bitcast.10.me_ref, bf16[3,1280,512]{2,1,0:T(8,128)(2,1)} %get-tuple-element.146.refs_0_.high_ref, bf16[1280,1024]{1,0:T(8,128)(2,1)} %get-tuple-element.135.refs_2_.refs_1_), custom_call_target="tpu_custom_call" | custom-call | flops 2013265920 | bytes 6553600 | tf_op jit(solution)/shard_map/pallas_call | solution.py:523
  294.7 3.3 collective-permute-done.13.refs_2_
  297.9 11.4 %shard_map.286 = (bf16[2,128,1280]{2,1,0:T(8,128)(2,1)}, bf16[2,128,1280]{2,1,0:T(8,128)(2,1)}, bf16[2,128,1280]{2,1,0:T(8,128)(2,1)}, bf16[2,128,1280]{2,1,0:T(8,128)(2,1)}) custom-call(s32[1]{0:T(128)} %bitcast.10.me_ref, bf16[3,1280,512]{2,1,0:T(8,128)(2,1)} %get-tuple-element.133.refs_0_.low_ref, bf16[1280,1024]{1,0:T(8,128)(2,1)} %get-tuple-element.138.refs_1_, ...), custom_call_target="tpu_custom_call" | custom-call | flops 3355443200 | bytes 9175040 | tf_op jit(solution)/shard_map/pallas_call | solution.py:548
  309.3 2.6 reduce-scatter.2.cloned.1.call-done
  315.3 7.0 %shard_map.287 = (bf16[2,128,768]{2,1,0:T(8,128)(2,1)}, bf16[2,128,768]{2,1,0:T(8,128)(2,1)}, bf16[2,128,768]{2,1,0:T(8,128)(2,1)}, bf16[2,128,768]{2,1,0:T(8,128)(2,1)}) custom-call(s32[1]{0:T(128)} %bitcast.10.me_ref, bf16[3,1280,512]{2,1,0:T(8,128)(2,1)} %get-tuple-element.146.refs_0_.high_ref, bf16[1280,1024]{1,0:T(8,128)(2,1)} %get-tuple-element.135.refs_2_.refs_1_, ...), custom_call_target="tpu_custom_call" | custom-call | flops 2013265920 | bytes 6553600 | tf_op jit(solution)/shard_map/pallas_call | solution.py:548
  324.7 6.4 %collective-permute-done.14.a_got = bf16[2,128,1280]{2,1,0:T(8,128)(2,1)S(1)} collective-permute-done((bf16[2,128,1280]{2,1,0:T(8,128)(2,1)}, bf16[2,128,1280]{2,1,0:T(8,128)(2,1)S(1)}, u32[]{:S(2)}, u32[]{:S(2)}) %collective-permute-start.14) | collective-permute-done | bytes 655392 | tf_op jit(solution)/shard_map/ppermute | solution.py:830
  333.3 2.8 shard_map.288
  336.1 22.8 %shard_map.289 = (bf16[1280,1024]{1,0:T(8,128)(2,1)}, f32[1,1024]{1,0:T(1,128)}, f32[1,1024]{1,0:T(1,128)}) custom-call(s32[1]{0:T(128)} %bitcast.2.start_ref, bf16[3,1280,512]{2,1,0:T(8,128)(2,1)} %get-tuple-element.133.refs_0_.low_ref, bf16[3,1280,512]{2,1,0:T(8,128)(2,1)} %get-tuple-element.146.refs_0_.high_ref, ...), custom_call_target="tpu_custom_call" | custom-call | tf_op jit(solution)/shard_map/pallas_call | solution.py:768
  361.1 2.3 shard_map.291
  369.6 2.2 shard_map.290
  373.4 20.1 %shard_map.292 = bf16[1280,1024]{1,0:T(8,128)(2,1)} custom-call(s32[1]{0:T(128)} %bitcast.2.start_ref, bf16[1280,4096]{1,0:T(8,128)(2,1)} %get-tuple-element.167.activ_ref, bf16[4096,1024]{1,0:T(8,128)(2,1)} %all-gather.5.cloned.1.call-done.w_ref, f32[1280,1024]{1,0:T(8,128)} %get-tuple-element.131.middle_ref, f32[1,1024]{1,0:T(1,128)} %bitcast.61), custom_call_target="tpu_custom_call" | custom-call | tf_op jit(solution)/shard_map/pallas_call | solution.py:794
  393.5 6.3 %collective-permute-done.25.got = bf16[64,2560]{1,0:T(8,128)(2,1)S(1)} collective-permute-done((bf16[64,2560]{1,0:T(8,128)(2,1)}, bf16[64,2560]{1,0:T(8,128)(2,1)S(1)}, u32[]{:S(2)}, u32[]{:S(2)}) %collective-permute-start.25) | collective-permute-done | bytes 327712 | tf_op jit(solution)/shard_map/ppermute | solution.py:834
  400.5 1.8 shard_map.293
  405.0 2.7 collective-permute-done.21
  409.7 2.0 shard_map.295
  411.8 3.4 collective-permute-start.31
  415.9 1.7 shard_map.294.low_own
  418.0 4.5 collective-permute-done.23
  422.6 1.7 collective-permute-start.24
  424.3 2.8 collective-permute-done.24
  427.7 3.8 shard_map.296
  432.2 1.7 shard_map.297
  433.9 1.7 collective-permute-start.32
  436.3 3.6 collective-permute-done.32.got
  443.8 1.8 collective-permute-start.28
  445.5 2.5 collective-permute-done.33.high_next
  448.9 3.3 collective-permute-start.34
  452.8 2.3 collective-permute-done.28.low_far
  455.1 2.5 collective-permute-done.34.high_far
  458.3 2.7 shard_map.299
  (212 shorter events, 53.6 us)
Async XLA Ops:
  7.2 99.4 %all-gather.3.cloned.1.call-start = ((), (), s32[]{:S(2)}) async-start(), calls=%async_computation.1 | async-start | bytes 11796480 | tf_op jit(solution)/shard_map/all_gather | solution.py:864
  7.2 20.8 %collective-permute-start.4 = (bf16[128,3072]{1,0:T(8,128)(2,1)}, bf16[128,3072]{1,0:T(8,128)(2,1)S(1)}, u32[]{:S(2)}, u32[]{:S(2)}) collective-permute-start(bf16[128,3072]{1,0:T(8,128)(2,1)} %refs_0_), channel_id=1, source_target_pairs={{0,2},{1,3},{2,0},{3,1},{4,6},{5,7},{6,4},{7,5},{8,10},{9,11},{10,... | collective-permute-start | bytes 2359304 | tf_op jit(solution)/shard_map/ppermute | solution.py:830
  10.2 19.2 %collective-permute-start.5 = (bf16[128,3072]{1,0:T(8,128)(2,1)}, bf16[128,3072]{1,0:T(8,128)(2,1)S(1)}, u32[]{:S(2)}, u32[]{:S(2)}) collective-permute-start(bf16[128,3072]{1,0:T(8,128)(2,1)} %refs_0_), channel_id=1, source_target_pairs={{0,4},{1,5},{2,6},{3,7},{4,0},{5,1},{6,2},{7,3},{8,12},{9,13},{10,... | collective-permute-start | bytes 2359304 | tf_op jit(solution)/shard_map/ppermute | solution.py:830
  26.6 24.7 %copy-start.27 = (f32[32,256,1]{1,0,2:T(8,128)S(1)}, f32[32,256,1]{1,0,2:T(8,128)}, u32[]{:S(2)}) copy-start(f32[32,256,1]{1,0,2:T(8,128)} %constant.39) | copy-start | bytes 98308
  28.0 26.7 %copy-start.17 = (bf16[128,3072]{1,0:T(8,128)(2,1)}, bf16[128,3072]{1,0:T(8,128)(2,1)S(1)}, u32[]{:S(2)}) copy-start(bf16[128,3072]{1,0:T(8,128)(2,1)S(1)} %collective-permute-done.4.refs_2_) | copy-start | bytes 2359300
  29.4 25.2 %copy-start.18 = (bf16[128,3072]{1,0:T(8,128)(2,1)}, bf16[128,3072]{1,0:T(8,128)(2,1)S(1)}, u32[]{:S(2)}) copy-start(bf16[128,3072]{1,0:T(8,128)(2,1)S(1)} %collective-permute-done.5.refs_3_) | copy-start | bytes 2359300
  29.5 9.7 %collective-permute-start.6 = (bf16[64,3072]{1,0:T(8,128)(2,1)S(1)}, bf16[64,3072]{1,0:T(8,128)(2,1)S(1)}, u32[]{:S(2)}, u32[]{:S(2)}) collective-permute-start(bf16[64,3072]{1,0:T(8,128)(2,1)S(1)} %slice.72), channel_id=1, source_target_pairs={{0,4},{1,5},{2,6},{3,7},{4,0},{5,1},{6,2},{7,3},{8,12},{9,13},{10,... | collective-permute-start | bytes 1179656 | tf_op jit(solution)/shard_map/ppermute | solution.py:830
  31.1 9.6 %collective-permute-start.7 = (bf16[64,3072]{1,0:T(8,128)(2,1)S(1)}, bf16[64,3072]{1,0:T(8,128)(2,1)}, u32[]{:S(2)}, u32[]{:S(2)}) collective-permute-start(bf16[64,3072]{1,0:T(8,128)(2,1)S(1)} %slice.73), channel_id=1, source_target_pairs={{0,2},{1,3},{2,0},{3,1},{4,6},{5,7},{6,4},{7,5},{8,10},{9,11},{10,... | collective-permute-start | bytes 1179656 | tf_op jit(solution)/shard_map/ppermute | solution.py:830
  40.7 119.9 %all-gather.5.cloned.1.call-start = ((), (), s32[]{:S(2)}) async-start(), calls=%async_computation.2 | async-start | bytes 9437184 | tf_op jit(solution)/shard_map/all_gather | solution.py:864
  41.2 1.2 collective-permute-start
  42.4 3.7 collective-permute-start.1
  46.1 3.8 collective-permute-start.2
  46.7 5.4 %collective-permute-start.3 = (bf16[128,3072]{1,0:T(8,128)(2,1)}, bf16[128,3072]{1,0:T(8,128)(2,1)S(1)}, u32[]{:S(2)}, u32[]{:S(2)}) collective-permute-start(bf16[128,3072]{1,0:T(8,128)(2,1)} %refs_0_), channel_id=1, source_target_pairs={{0,1},{1,0},{2,3},{3,2},{4,5},{5,4},{6,7},{7,6},{8,9},{9,8},{10,11... | collective-permute-start | bytes 2359304 | tf_op jit(solution)/shard_map/ppermute | solution.py:830
  50.0 4.4 collective-permute-start.8
  50.0 4.7 collective-permute-start.9
  50.7 3.2 collective-permute-start.10
  50.8 3.6 collective-permute-start.11
  106.6 205.3 %reduce-scatter.2.cloned.1.call-start = ((), (), s32[]{:S(2)}) async-start(), calls=%async_computation.3 | async-start | bytes 18874368 | tf_op jit(solution)/shard_map/reduce_scatter | solution.py:906
  195.7 231.9 %all-reduce.2.cloned.1.call-start = ((), (), s32[]{:S(2)}) async-start(), calls=%async_computation.4 | async-start | bytes 4194304 | tf_op jit(solution)/shard_map/psum | solution.py:907
  259.2 5.1 %collective-permute-start.12 = (bf16[512,2560]{1,0:T(8,128)(2,1)}, bf16[512,2560]{1,0:T(8,128)(2,1)S(1)}, u32[]{:S(2)}, u32[]{:S(2)}) collective-permute-start(bf16[512,2560]{1,0:T(8,128)(2,1)} %shard_map.283), channel_id=1, source_target_pairs={{0,1},{1,0},{2,3},{3,2},{4,5},{5,4},{6,7},{7,6},{8,9},{9,8},{10,11... | collective-permute-start | bytes 7864328 | tf_op jit(solution)/shard_map/ppermute | solution.py:830
  264.3 23.1 %copy-start.1 = (bf16[512,2560]{1,0:T(8,128)(2,1)}, bf16[512,2560]{1,0:T(8,128)(2,1)S(1)}, u32[]{:S(2)}) copy-start(bf16[512,2560]{1,0:T(8,128)(2,1)S(1)} %collective-permute-done.12.refs_4_) | copy-start | bytes 7864324
  294.2 21.0 %copy-start.30 = (f32[4,2,256]{2,1,0:T(2,128)S(1)}, f32[4,2,256]{2,1,0:T(2,128)}, u32[]{:S(2)}) copy-start(f32[4,2,256]{2,1,0:T(2,128)} %get-tuple-element.175) | copy-start | bytes 24580
  294.2 3.7 collective-permute-start.13
  313.1 17.9 %collective-permute-start.14 = (bf16[2,128,1280]{2,1,0:T(8,128)(2,1)}, bf16[2,128,1280]{2,1,0:T(8,128)(2,1)S(1)}, u32[]{:S(2)}, u32[]{:S(2)}) collective-permute-start(bf16[2,128,1280]{2,1,0:T(8,128)(2,1)} %get-tuple-element.142), channel_id=1, source_target_pairs={{0,2},{1,3},{2,0},{3,1},{4,6},{5,7},{6,4},{7,5},{8,10},{9,11},{10,... | collective-permute-start | bytes 1966088 | tf_op jit(solution)/shard_map/ppermute | solution.py:830
  314.6 17.9 %collective-permute-start.15 = (bf16[2,128,1280]{2,1,0:T(8,128)(2,1)}, bf16[2,128,1280]{2,1,0:T(8,128)(2,1)S(1)}, u32[]{:S(2)}, u32[]{:S(2)}) collective-permute-start(bf16[2,128,1280]{2,1,0:T(8,128)(2,1)} %get-tuple-element.144), channel_id=1, source_target_pairs={{0,4},{1,5},{2,6},{3,7},{4,0},{5,1},{6,2},{7,3},{8,12},{9,13},{10,... | collective-permute-start | bytes 1966088 | tf_op jit(solution)/shard_map/ppermute | solution.py:830
  322.3 36.7 %collective-permute-start.18 = (bf16[2,128,768]{2,1,0:T(8,128)(2,1)}, bf16[2,128,768]{2,1,0:T(8,128)(2,1)S(1)}, u32[]{:S(2)}, u32[]{:S(2)}) collective-permute-start(bf16[2,128,768]{2,1,0:T(8,128)(2,1)} %get-tuple-element.159), channel_id=1, source_target_pairs={{0,2},{1,3},{2,0},{3,1},{4,6},{5,7},{6,4},{7,5},{8,10},{9,11},{10,... | collective-permute-start | bytes 1179656 | tf_op jit(solution)/shard_map/ppermute | solution.py:830
  324.0 35.0 %collective-permute-start.19 = (bf16[2,128,768]{2,1,0:T(8,128)(2,1)}, bf16[2,128,768]{2,1,0:T(8,128)(2,1)S(1)}, u32[]{:S(2)}, u32[]{:S(2)}) collective-permute-start(bf16[2,128,768]{2,1,0:T(8,128)(2,1)} %get-tuple-element.161), channel_id=1, source_target_pairs={{0,4},{1,5},{2,6},{3,7},{4,0},{5,1},{6,2},{7,3},{8,12},{9,13},{10,... | collective-permute-start | bytes 1179656 | tf_op jit(solution)/shard_map/ppermute | solution.py:830
  336.1 22.9 %copy-start.46 = (bf16[128,1280]{1,0:T(8,128)(2,1)S(1)}, bf16[128,1280]{1,0:T(8,128)(2,1)}, u32[]{:S(2)}) copy-start(bf16[128,1280]{1,0:T(8,128)(2,1)} %get-tuple-element.151) | copy-start | bytes 983044
  336.1 23.6 %copy-start.45 = (bf16[128,1280]{1,0:T(8,128)(2,1)S(1)}, bf16[128,1280]{1,0:T(8,128)(2,1)}, u32[]{:S(2)}) copy-start(bf16[128,1280]{1,0:T(8,128)(2,1)} %get-tuple-element.153) | copy-start | bytes 983044
  336.1 30.7 %copy-start.33 = (f32[1,1024]{1,0:T(1,128)S(1)}, f32[1,1024]{1,0:T(1,128)}, u32[]{:S(2)}) copy-start(f32[1,1024]{1,0:T(1,128)} %get-tuple-element.170) | copy-start | bytes 12292
  359.0 9.2 %collective-permute-start.16 = (bf16[128,1280]{1,0:T(8,128)(2,1)S(1)}, bf16[128,1280]{1,0:T(8,128)(2,1)S(1)}, u32[]{:S(2)}, u32[]{:S(2)}) collective-permute-start(bf16[128,1280]{1,0:T(8,128)(2,1)S(1)} %copy-done.46), channel_id=1, source_target_pairs={{0,4},{1,5},{2,6},{3,7},{4,0},{5,1},{6,2},{7,3},{8,12},{9,13},{10,... | collective-permute-start | bytes 983048 | tf_op jit(solution)/shard_map/ppermute | solution.py:830
  359.7 9.2 %collective-permute-start.17 = (bf16[128,1280]{1,0:T(8,128)(2,1)S(1)}, bf16[128,1280]{1,0:T(8,128)(2,1)S(1)}, u32[]{:S(2)}, u32[]{:S(2)}) collective-permute-start(bf16[128,1280]{1,0:T(8,128)(2,1)S(1)} %copy-done.45), channel_id=1, source_target_pairs={{0,2},{1,3},{2,0},{3,1},{4,6},{5,7},{6,4},{7,5},{8,10},{9,11},{10,... | collective-permute-start | bytes 983048 | tf_op jit(solution)/shard_map/ppermute | solution.py:830
  363.5 45.5 %collective-permute-start.29 = (bf16[128,768]{1,0:T(8,128)(2,1)}, bf16[128,768]{1,0:T(8,128)(2,1)S(1)}, u32[]{:S(2)}, u32[]{:S(2)}) collective-permute-start(bf16[128,768]{1,0:T(8,128)(2,1)} %get-tuple-element.181), channel_id=1, source_target_pairs={{0,4},{1,5},{2,6},{3,7},{4,0},{5,1},{6,2},{7,3},{8,12},{9,13},{10,... | collective-permute-start | bytes 589832 | tf_op jit(solution)/shard_map/ppermute | solution.py:830
  364.1 44.9 %collective-permute-start.30 = (bf16[128,768]{1,0:T(8,128)(2,1)}, bf16[128,768]{1,0:T(8,128)(2,1)S(1)}, u32[]{:S(2)}, u32[]{:S(2)}) collective-permute-start(bf16[128,768]{1,0:T(8,128)(2,1)} %get-tuple-element.183), channel_id=1, source_target_pairs={{0,2},{1,3},{2,0},{3,1},{4,6},{5,7},{6,4},{7,5},{8,10},{9,11},{10,... | collective-permute-start | bytes 589832 | tf_op jit(solution)/shard_map/ppermute | solution.py:830
  371.9 28.0 %collective-permute-start.25 = (bf16[64,2560]{1,0:T(8,128)(2,1)}, bf16[64,2560]{1,0:T(8,128)(2,1)S(1)}, u32[]{:S(2)}, u32[]{:S(2)}) collective-permute-start(bf16[64,2560]{1,0:T(8,128)(2,1)} %get-tuple-element.176), channel_id=1, source_target_pairs={{0,8},{8,0},{16,24},{24,16},{1,9},{9,1},{17,25},{25,17},{2,10},{10... | collective-permute-start | bytes 983048 | tf_op jit(solution)/shard_map/ppermute | solution.py:834
  402.4 12.8 %collective-permute-start.26 = (bf16[32,2560]{1,0:T(8,128)(2,1)}, bf16[32,2560]{1,0:T(8,128)(2,1)S(1)}, u32[]{:S(2)}, u32[]{:S(2)}) collective-permute-start(bf16[32,2560]{1,0:T(8,128)(2,1)} %get-tuple-element.180), channel_id=1, source_target_pairs={{0,16},{8,24},{16,0},{24,8},{1,17},{9,25},{17,1},{25,9},{2,18},{10... | collective-permute-start | bytes 491528 | tf_op jit(solution)/shard_map/ppermute | solution.py:834
  402.4 1.3 collective-permute-start.20
  403.7 4.0 collective-permute-start.21
  407.7 10.0 %collective-permute-start.22 = (f32[8,1216]{1,0:T(8,128)S(1)}, f32[8,1216]{1,0:T(8,128)S(1)}, u32[]{:S(2)}, u32[]{:S(2)}) collective-permute-start(f32[8,1216]{1,0:T(8,128)S(1)} %add.27), channel_id=1, source_target_pairs={{0,4},{1,5},{2,6},{3,7},{4,0},{5,1},{6,2},{7,3},{8,12},{9,13},{10,... | collective-permute-start | bytes 116744 | tf_op jit(solution)/shard_map/ppermute | solution.py:830
  411.8 19.8 %collective-permute-start.31 = (bf16[64,1536]{1,0:T(8,128)(2,1)}, bf16[64,1536]{1,0:T(8,128)(2,1)S(1)}, u32[]{:S(2)}, u32[]{:S(2)}) collective-permute-start(bf16[64,1536]{1,0:T(8,128)(2,1)} %get-tuple-element.189), channel_id=1, source_target_pairs={{0,8},{8,0},{16,24},{24,16},{1,9},{9,1},{17,25},{25,17},{2,10},{10... | collective-permute-start | bytes 589832 | tf_op jit(solution)/shard_map/ppermute | solution.py:834
  417.6 26.1 %copy-start.4 = (bf16[32,2560]{1,0:T(8,128)(2,1)S(1)}, bf16[32,2560]{1,0:T(8,128)(2,1)}, u32[]{:S(2)}) copy-start(bf16[32,2560]{1,0:T(8,128)(2,1)} %shard_map.294.low_own) | copy-start | bytes 491524
  417.6 26.1 %collective-permute-start.27 = (bf16[32,2560]{1,0:T(8,128)(2,1)}, bf16[32,2560]{1,0:T(8,128)(2,1)S(1)}, u32[]{:S(2)}, u32[]{:S(2)}) collective-permute-start(bf16[32,2560]{1,0:T(8,128)(2,1)} %shard_map.294.low_own), channel_id=1, source_target_pairs={{0,16},{8,24},{16,0},{24,8},{1,17},{9,25},{17,1},{25,9},{2,18},{10... | collective-permute-start | bytes 491528 | tf_op jit(solution)/shard_map/ppermute | solution.py:834
  417.7 4.9 %collective-permute-start.23 = (f32[1,1216]{1,0:T(1,128)S(1)}, f32[1,1216]{1,0:T(1,128)S(1)}, u32[]{:S(2)}, u32[]{:S(2)}) collective-permute-start(f32[1,1216]{1,0:T(1,128)S(1)} %dynamic-slice_add_fusion), channel_id=1, source_target_pairs={{0,8},{8,0},{16,24},{24,16},{1,9},{9,1},{17,25},{25,17},{2,10},{10... | collective-permute-start | bytes 14600 | tf_op jit(solution)/shard_map/ppermute | solution.py:834
  422.6 4.5 collective-permute-start.24
  433.9 6.0 %collective-permute-start.32 = (bf16[32,1536]{1,0:T(8,128)(2,1)}, bf16[32,1536]{1,0:T(8,128)(2,1)S(1)}, u32[]{:S(2)}, u32[]{:S(2)}) collective-permute-start(bf16[32,1536]{1,0:T(8,128)(2,1)} %get-tuple-element.196), channel_id=1, source_target_pairs={{0,16},{8,24},{16,0},{24,8},{1,17},{9,25},{17,1},{25,9},{2,18},{10... | collective-permute-start | bytes 294920 | tf_op jit(solution)/shard_map/ppermute | solution.py:834
  442.2 5.8 %collective-permute-start.33 = (bf16[32,1536]{1,0:T(8,128)(2,1)}, bf16[32,1536]{1,0:T(8,128)(2,1)S(1)}, u32[]{:S(2)}, u32[]{:S(2)}) collective-permute-start(bf16[32,1536]{1,0:T(8,128)(2,1)} %shard_map.298.high_own), channel_id=1, source_target_pairs={{0,16},{8,24},{16,0},{24,8},{1,17},{9,25},{17,1},{25,9},{2,18},{10... | collective-permute-start | bytes 294920 | tf_op jit(solution)/shard_map/ppermute | solution.py:834
  443.8 11.3 %collective-permute-start.28 = (bf16[64,2560]{1,0:T(8,128)(2,1)S(1)}, bf16[64,2560]{1,0:T(8,128)(2,1)S(1)}, u32[]{:S(2)}, u32[]{:S(2)}) collective-permute-start(bf16[64,2560]{1,0:T(8,128)(2,1)S(1)} %pad_maximum_fusion), channel_id=1, source_target_pairs={{0,8},{8,0},{16,24},{24,16},{1,9},{9,1},{17,25},{25,17},{2,10},{10... | collective-permute-start | bytes 983048 | tf_op jit(solution)/shard_map/ppermute | solution.py:834
  448.9 8.6 %collective-permute-start.34 = (bf16[64,1536]{1,0:T(8,128)(2,1)S(1)}, bf16[64,1536]{1,0:T(8,128)(2,1)S(1)}, u32[]{:S(2)}, u32[]{:S(2)}) collective-permute-start(bf16[64,1536]{1,0:T(8,128)(2,1)S(1)} %pad_maximum_fusion.1), channel_id=1, source_target_pairs={{0,8},{8,0},{16,24},{24,16},{1,9},{9,1},{17,25},{25,17},{2,10},{10... | collective-permute-start | bytes 589832 | tf_op jit(solution)/shard_map/ppermute | solution.py:834
  (39 other events, 293.6 us)
Sparse Core Ops, SparseCore 0:
  40.8 62.6 all-gather.2
  106.7 53.7 all-gather.4
  195.9 115.9 reduce-scatter.1
  314.1 94.1 all-reduce.1
